TPU v7x, 512 devices: a whole 4x8x8 slice. The times are simulated.
512 devices in a mesh: chan: 64 (over y, z_hi, core), day: 8 (over x, z_lo).
Axes of the slice: x: 4, y: 8, z: 8 (z_hi: 4, z_lo: 2; z = z_hi * 2 + z_lo), core: 2. Of those that a mesh axis runs over, the one named last changes fastest.
Arguments:
- recordings: bfloat16 [8, 4096, 8, 1024], P('day', 'chan'), may hold values from -6 to 6
- good_windows: int32 [8, 4096, 8], P('day', 'chan'), may hold values 0 or 1
- response: float32 [256], replicated, may hold values from 0.3 to 3
Outputs:
- correlations: float32 [4096, 2, 64, 128], P(('chan', 'day'))
All inputs are finite; a program needn't handle non-finite values. No bound on the sum of `good_windows` on one device may be relied on, other than what follows from the above.
Results may differ from a plain program's by a relative error of at most 0.0076.
Values may be sent and summed in bfloat16 or wider, within the bound.
No kernel may reach another device: no remote copies, remote signals or barrier semaphores. Data moves between devices by JAX's collectives and lax.ppermute only.
A program may use at most 64 MiB of HBM per device.

v0:
```python
import math

import jax
import jax.numpy as jnp
from jax import lax
from jax.sharding import PartitionSpec as P

FIRST_BIN = 4
L = 128
ROUNDS = 2


def from_behind(value, axis, steps):
    count = lax.axis_size(axis)
    pairs = [(source, (source + steps) % count) for source in range(count)]
    return lax.ppermute(value, axis, pairs)


def dft_table(samples, bin_count, first_bin):
    sample_index = jnp.arange(samples, dtype=jnp.int32)
    bin_index = jnp.arange(bin_count, dtype=jnp.int32) + first_bin
    phase_int = jnp.mod(sample_index[:, None] * bin_index[None, :], samples)
    phase = phase_int.astype(jnp.float32) * (2.0 * math.pi / samples)
    return jnp.concatenate([jnp.cos(phase), -jnp.sin(phase)], axis=1).astype(jnp.bfloat16)


def paired_lag_table(samples, bin_count, first_bin, lag_count):
    bin_index = jnp.arange(bin_count, dtype=jnp.int32) + first_bin
    shift_index = jnp.arange(lag_count, dtype=jnp.int32) - lag_count // 2
    phase_int = jnp.mod(bin_index[:, None] * shift_index[None, :], samples)
    phase = phase_int.astype(jnp.float32) * (2.0 * math.pi / samples)
    paired = jnp.stack([jnp.cos(phase), -jnp.sin(phase)], axis=1)
    return paired.reshape(2 * bin_count, lag_count).astype(jnp.bfloat16)


def band_spectra(recordings, good_windows, response):
    days, chans, windows, samples = recordings.shape
    bin_count = response.shape[0]
    values = recordings.astype(jnp.float32)
    power = jnp.mean(values * values, axis=-1, keepdims=True)
    normed = (values * lax.rsqrt(power + 1e-06)).astype(jnp.bfloat16)
    flat = normed.reshape(-1, samples)
    spectra = jnp.dot(
        flat, dft_table(samples, bin_count, FIRST_BIN), preferred_element_type=jnp.float32
    )
    spectra = spectra.reshape(days, chans, windows, 2 * bin_count)
    weight = good_windows.astype(jnp.float32)[..., None] * jnp.concatenate([response, response])
    spectra = (spectra * weight).astype(jnp.bfloat16)
    spectra = spectra.reshape(days, chans, windows, 2, bin_count)
    spectra = jnp.transpose(spectra, (4, 0, 2, 3, 1))
    return spectra.reshape(bin_count, days * windows, 2, chans)


def cross_lags(mine, partner, table):
    bin_count, pairs, _, chans = mine.shape
    rotated = jnp.stack([mine[:, :, 1], -mine[:, :, 0]], axis=2)
    left_side = jnp.stack([mine, rotated], axis=3).reshape(bin_count, 2 * pairs, 2 * chans)
    right_side = partner.reshape(bin_count, 2 * pairs, chans)
    cross = lax.dot_general(
        left_side, right_side, (((1,), (1,)), ((0,), (0,))), preferred_element_type=jnp.float32
    )
    cross = cross.astype(jnp.bfloat16).reshape(2 * bin_count, chans * chans)
    lag_sums = lax.dot_general(
        cross, table, (((0,), (0,)), ((), ())), preferred_element_type=jnp.float32
    )
    return lag_sums.reshape(chans, chans, -1)


def shards(recordings, good_windows, response):
    spectra = band_spectra(recordings, good_windows, response)
    table = paired_lag_table(recordings.shape[-1], response.shape[0], FIRST_BIN, L)
    lag_blocks = []
    current = spectra
    for round_index in range(ROUNDS):
        current = from_behind(current, "chan", -1)
        lag_sums = cross_lags(spectra, current, table)
        lag_blocks.append(lag_sums)
    stacked = jnp.stack(lag_blocks, axis=1)
    stacked = lax.psum_scatter(stacked, "day", scatter_dimension=0, tiled=True)
    return stacked


def solution(mesh):
    in_specs = (P("day", "chan", None, None), P("day", "chan", None), P())
    out_specs = P(("chan", "day"), None, None, None)
    return jax.shard_map(shards, mesh=mesh, in_specs=in_specs, out_specs=out_specs, check_vma=False)
```

profile of v0, /device:TPU:1, one launch (start us, length us, event | category | flops | bytes accessed | tf_op | source)
XLA Modules:
  0.0 229.8 jit_solution(6532417648562623504)
XLA Ops:
  6.5 0.0 reduce-scatter.5.cloned.1.call-start
  6.5 4.4 %cosine_convert_fusion = (bf16[1024,256]{1,0:T(8,128)(2,1)S(1)}, bf16[1024,256]{1,0:T(8,128)(2,1)S(1)}) fusion(s32[256]{0:T(256)S(1)} %iota_add_fusion), kind=kLoop, calls=%fused_computation.24 | loop fusion | flops 4456448 | bytes 1049600 | tf_op jit(solution)/shard_map/convert.2
  11.0 1.5 fusion
  12.5 0.1 copy.72
  12.5 0.1 copy.73
  12.6 0.7 convert_bitcast_fusion
  13.3 0.1 copy.74
  13.4 0.8 pad_maximum_fusion.3
  14.2 2.0 fusion.2
  16.2 0.2 copy.95
  16.3 8.8 %collective-permute-start = (bf16[256,8,2,64]{0,3,2,1:T(8,128)(2,1)S(1)}, bf16[256,8,2,64]{0,3,2,1:T(8,128)(2,1)}, u32[]{:S(2)}, u32[]{:S(2)}) collective-permute-start(bf16[256,8,2,64]{0,3,2,1:T(8,128)(2,1)S(1)} %bitcast.61), channel_id=1, source_target_pairs={{0,504},{8,0},{16,8},{24,16},{32,24},{40,32},{48,40},{56,48},{64,5... | collective-permute-start | bytes 1572872 | tf_op jit(solution)/shard_map/ppermute | solution.py:16
  25.2 0.2 copy.76
  25.3 0.1 maximum_bitcast_fusion.2
  25.4 0.1 pad_maximum_fusion.1
  25.5 1.1 copy.78
  26.6 0.6 cosine_convert_fusion.1
  27.2 0.1 copy.81
  27.4 10.6 %collective-permute-done = bf16[256,8,2,64]{0,3,2,1:T(8,128)(2,1)} collective-permute-done((bf16[256,8,2,64]{0,3,2,1:T(8,128)(2,1)S(1)}, bf16[256,8,2,64]{0,3,2,1:T(8,128)(2,1)}, u32[]{:S(2)}, u32[]{:S(2)}) %collective-permute-start) | collective-permute-done | bytes 524320 | tf_op jit(solution)/shard_map/ppermute | solution.py:16
  37.9 2.5 %copy.77 = bf16[256,8,2,64]{3,2,1,0:T(2,128)(2,1)S(1)} copy(bf16[256,8,2,64]{0,3,2,1:T(8,128)(2,1)} %collective-permute-done) | data formatting | bytes 1048576 | tf_op jit(solution)/shard_map/ppermute | solution.py:16
  40.4 4.1 %collective-permute-start.1 = (bf16[256,8,2,64]{0,3,2,1:T(8,128)(2,1)}, bf16[256,8,2,64]{0,3,2,1:T(8,128)(2,1)}, u32[]{:S(2)}, u32[]{:S(2)}) collective-permute-start(bf16[256,8,2,64]{0,3,2,1:T(8,128)(2,1)} %collective-permute-done), channel_id=1, source_target_pairs={{0,504},{8,0},{16,8},{24,16},{32,24},{40,32},{48,40},{56,48},{64,5... | collective-permute-start | bytes 1572872 | tf_op jit(solution)/shard_map/ppermute | solution.py:16
  44.5 3.3 %convolution_convert_fusion.1 = bf16[256,128,64]{1,2,0:T(8,128)(2,1)} fusion(bf16[256,16,128]{2,1,0:T(8,128)(2,1)S(1)} %copy.78, bf16[256,16,64]{2,1,0:T(8,128)(2,1)S(1)} %bitcast.59), kind=kOutput, calls=%fused_computation.3 | convolution fusion | flops 69206016 | bytes 5767168 | tf_op jit(solution)/shard_map/dot_general | solution.py:59
  47.8 8.4 %copy.79 = bf16[256,128,64]{2,1,0:T(8,128)(2,1)} copy(bf16[256,128,64]{1,2,0:T(8,128)(2,1)} %convolution_convert_fusion.1) | data formatting | bytes 8388608 | tf_op jit(solution)/shard_map/convert_element_type | solution.py:62
  56.2 12.0 %reshape.213 = bf16[512,4096]{1,0:T(8,128)(2,1)} reshape(bf16[256,128,64]{2,1,0:T(8,128)(2,1)} %copy.79) | data formatting | bytes 8388608 | tf_op jit(solution)/shard_map/reshape | solution.py:62
  68.2 6.5 %copy.80 = bf16[4096,512]{1,0:T(8,128)(2,1)} copy(bf16[4096,512]{0,1:T(8,128)(2,1)} %bitcast.52) | data formatting | bytes 8388608 | tf_op jit(solution)/shard_map/dot_general | solution.py:63
  74.7 3.4 %convolution_bitcast_fusion.1 = f32[64,1,64,128]{3,2,0,1:T(8,128)S(1)} fusion(bf16[64,64,512]{2,1,0:T(8,128)(2,1)} %bitcast.56, bf16[512,128,1]{1,0,2:T(8,128)(2,1)S(1)} %bitcast.65), kind=kOutput, calls=%fused_computation.9 | convolution fusion | flops 536870912 | bytes 6422528 | tf_op jit(solution)/shard_map/dot_general | solution.py:63
  78.1 0.0 collective-permute-done.1
  78.1 3.6 %copy.82 = bf16[256,8,2,64]{3,2,1,0:T(2,128)(2,1)} copy(bf16[256,8,2,64]{0,3,2,1:T(8,128)(2,1)} %collective-permute-done.1) | data formatting | bytes 1048576 | tf_op jit(solution)/shard_map/ppermute | solution.py:16
  81.8 4.6 %convolution_convert_fusion = bf16[256,128,64]{1,2,0:T(8,128)(2,1)} fusion(bf16[256,16,128]{2,1,0:T(8,128)(2,1)S(1)} %copy.78, bf16[256,16,64]{2,1,0:T(8,128)(2,1)} %bitcast.60), kind=kOutput, calls=%fused_computation.2 | convolution fusion | flops 69206016 | bytes 5767168 | tf_op jit(solution)/shard_map/dot_general | solution.py:59
  86.3 8.4 %copy.84 = bf16[256,128,64]{2,1,0:T(8,128)(2,1)} copy(bf16[256,128,64]{1,2,0:T(8,128)(2,1)} %convolution_convert_fusion) | data formatting | bytes 8388608 | tf_op jit(solution)/shard_map/convert_element_type | solution.py:62
  94.7 12.0 %reshape.216 = bf16[512,4096]{1,0:T(8,128)(2,1)} reshape(bf16[256,128,64]{2,1,0:T(8,128)(2,1)} %copy.84) | data formatting | bytes 8388608 | tf_op jit(solution)/shard_map/reshape | solution.py:62
  106.7 6.5 %copy.85 = bf16[4096,512]{1,0:T(8,128)(2,1)} copy(bf16[4096,512]{0,1:T(8,128)(2,1)} %bitcast.53) | data formatting | bytes 8388608 | tf_op jit(solution)/shard_map/dot_general | solution.py:63
  113.2 3.4 %convolution_bitcast_fusion = f32[64,1,64,128]{3,2,0,1:T(8,128)S(1)} fusion(bf16[64,64,512]{2,1,0:T(8,128)(2,1)} %bitcast.55, bf16[512,128,1]{1,0,2:T(8,128)(2,1)S(1)} %bitcast.66), kind=kOutput, calls=%fused_computation.8 | convolution fusion | flops 536870912 | bytes 6422528 | tf_op jit(solution)/shard_map/dot_general | solution.py:63
  116.6 0.6 pad_maximum_fusion
  117.2 0.6 copy.88
  117.8 4.3 %copy.94 = f32[8,8,128,128]{3,1,2,0:T(8,128)} copy(f32[8,8,128,128]{3,2,1,0:T(8,128)S(1)} %bitcast.57) | data formatting | bytes 8388608
  122.1 0.0 reduce-scatter.5.cloned.1.call-update
  122.1 98.9 %reduce-scatter.5.cloned.1.call-done = f32[8,16384]{1,0:T(8,128)} async-done(((f32[64,16384]{1,0:T(8,128)}), f32[8,16384]{1,0:T(8,128)}) %reduce-scatter.5.cloned.1.call-update) | async-done | bytes 524304
  221.0 1.9 copy.91
  (5 shorter events, 0.1 us)
Async XLA Ops:
  6.5 214.5 %reduce-scatter.5.cloned.1.call-start = ((), (), s32[]{:S(2)}) async-start(), calls=%async_computation.1 | async-start | bytes 4718592
  16.3 21.6 %collective-permute-start = (bf16[256,8,2,64]{0,3,2,1:T(8,128)(2,1)S(1)}, bf16[256,8,2,64]{0,3,2,1:T(8,128)(2,1)}, u32[]{:S(2)}, u32[]{:S(2)}) collective-permute-start(bf16[256,8,2,64]{0,3,2,1:T(8,128)(2,1)S(1)} %bitcast.61), channel_id=1, source_target_pairs={{0,504},{8,0},{16,8},{24,16},{32,24},{40,32},{48,40},{56,48},{64,5... | collective-permute-start | bytes 1572872 | tf_op jit(solution)/shard_map/ppermute | solution.py:16
  40.4 37.7 %collective-permute-start.1 = (bf16[256,8,2,64]{0,3,2,1:T(8,128)(2,1)}, bf16[256,8,2,64]{0,3,2,1:T(8,128)(2,1)}, u32[]{:S(2)}, u32[]{:S(2)}) collective-permute-start(bf16[256,8,2,64]{0,3,2,1:T(8,128)(2,1)} %collective-permute-done), channel_id=1, source_target_pairs={{0,504},{8,0},{16,8},{24,16},{32,24},{40,32},{48,40},{56,48},{64,5... | collective-permute-start | bytes 1572872 | tf_op jit(solution)/shard_map/ppermute | solution.py:16
Sparse Core Ops, SparseCore 0:
  122.2 98.7 reduce-scatter.4
where the time goes:
time: 231 us; the launch traced here: 230 us
  waiting for transfers between devices  109 us (47%)
  local copies, waits for them, and re-layouts  68.4 us (30%)
  matrix products  16.7 us (7%)
  between operations  13.5 us (6%)
  starting transfers between devices  12.8 us (6%)
  other arithmetic  8.78 us (4%)
    unnamed x2, waiting for transfers between devices  98.9 us
    reshape x2, local copies, waits for them, and re-layouts, cross_lags(): cross = cross.astype(jnp.bfloat16).reshape(2 * bin_count, chans * chans)  24.1 us
    convert_element_type x2, local copies, waits for them, and re-layouts, cross_lags(): cross = cross.astype(jnp.bfloat16).reshape(2 * bin_count, chans * chans)  16.7 us
    dot_general x2, local copies, waits for them, and re-layouts, cross_lags(): lax.dot_general(cross, table, (((0,), (0,)), ((), ())), preferred_element...  13 us
    ppermute x2, starting transfers between devices, from_behind(): return lax.ppermute(value, axis, pairs)  12.8 us
    ppermute x2, waiting for transfers between devices, from_behind(): return lax.ppermute(value, axis, pairs)  10.6 us
    dot_general x2, matrix products, cross_lags(): lax.dot_general(left_side, right_side, (((1,), (1,)), ((0,), (0,))), pref...  7.89 us
    dot_general x2, matrix products, cross_lags(): lax.dot_general(cross, table, (((0,), (0,)), ((), ())), preferred_element...  6.86 us
  transfers between devices with their start and end apart: 3, of which 2 were waited for; matrix products, arithmetic and copies ran while one was open for 16% of the time, Pallas kernels for 0%

commit v1 on v0

v1 whole, which is shorter than its diff:
```python
import functools
import math

import jax
import jax.numpy as jnp
import ml_dtypes
import numpy as np
from jax import lax
from jax.experimental import pallas as pl
from jax.experimental.pallas import tpu as pltpu
from jax.sharding import PartitionSpec as P

FIRST_BIN = 4
S = 1024
F = 256
L = 128
CB = 64
W = 8
DAYS = 8
FS = F // DAYS
VMEM = 40 * 1024 * 1024


def phase_table(product):
    phase = np.mod(product, S).astype(np.float32) * np.float32(2.0 * math.pi / S)
    return np.cos(phase), -np.sin(phase)


def dft_table():
    bins = np.arange(F) + FIRST_BIN
    re, im = phase_table(bins[:, None] * np.arange(S)[None, :])
    return np.concatenate([re, im], axis=0).astype(ml_dtypes.bfloat16)


def lag_table():
    bins = np.arange(F) + FIRST_BIN
    re, im = phase_table(bins[:, None] * (np.arange(L) - L // 2)[None, :])
    return np.concatenate([re, im], axis=0).astype(ml_dtypes.bfloat16)


def lower_half(shape):
    return lax.broadcasted_iota(jnp.int32, shape, 1) < CB


def spectra_kernel(x_ref, good_ref, resp_ref, table_ref, out_ref, xs, normed):
    for lane in range(S // 128):
        xs[lane] = x_ref[:, 128 * lane : 128 * (lane + 1)].astype(jnp.float32)
    for w in range(W):
        rows = pl.ds(w, CB, stride=W)
        v = jnp.concatenate([xs[lane, rows, :] for lane in range(S // 128)], axis=1)
        power = jnp.mean(v * v, axis=-1, keepdims=True)
        normed[pl.ds(w * CB, CB), :] = (v * lax.rsqrt(power + 1e-06)).astype(jnp.bfloat16)
    gain = jnp.transpose(jnp.broadcast_to(resp_ref[...], (2 * CB, F)))
    low = lower_half((F, 2 * CB))
    good = good_ref[...].astype(jnp.float32)
    for half in range(2):
        rows = normed[pl.ds(half * 4 * CB, 4 * CB), :]
        spectra = lax.dot_general(
            table_ref[...], rows, (((1,), (1,)), ((), ())), preferred_element_type=jnp.float32
        )
        for pair in range(2):
            w = 4 * half + 2 * pair
            mask = jnp.concatenate([good[w : w + 1, :], good[w + 1 : w + 2, :]], axis=1)
            weight = gain * mask
            cols = slice(2 * CB * pair, 2 * CB * (pair + 1))
            re = spectra[:F, cols] * weight
            im = spectra[F:, cols] * weight
            first = jnp.where(low, re, pltpu.roll(im, CB, 1))
            second = jnp.where(low, pltpu.roll(re, CB, 1), im)
            out_ref[:, w] = first.astype(jnp.bfloat16).reshape(DAYS, FS, 2 * CB)
            out_ref[:, w + 1] = second.astype(jnp.bfloat16).reshape(DAYS, FS, 2 * CB)


def cross_kernel(mine_ref, one_ref, two_ref, out_ref, wide):
    for at, ref in enumerate((mine_ref, one_ref, two_ref)):
        wide[at] = ref[...].astype(jnp.float32)
    low = lower_half((DAYS * W, 2 * CB))
    for f in range(FS):
        rows = pl.ds(f, DAYS * W, stride=FS)
        mine, one, two = wide[0, rows, :], wide[1, rows, :], wide[2, rows, :]
        turned = pltpu.roll(mine, CB, 1)
        left = jnp.concatenate([mine, jnp.where(low, turned, -turned)], axis=0)
        right = jnp.concatenate(
            [
                jnp.where(low, one, pltpu.roll(two, CB, 1)),
                jnp.where(low, pltpu.roll(one, CB, 1), two),
            ],
            axis=0,
        )
        cross = lax.dot_general(
            left.astype(jnp.bfloat16),
            right.astype(jnp.bfloat16),
            (((0,), (0,)), ((), ())),
            preferred_element_type=jnp.float32,
        )
        for k in range(DAYS):
            piece = jnp.concatenate([cross[8 * k : 8 * k + 8], cross[CB + 8 * k : CB + 8 * k + 8]], axis=0)
            out_ref[k, f] = piece.astype(jnp.bfloat16)


def lag_kernel(cross_ref, table_ref, out_ref, wide):
    wide[...] = cross_ref[...].astype(jnp.float32)
    for i in range(8):
        parts = [wide[pl.ds(c * 8 + i, F, stride=16), :] for c in range(2)]
        left = jnp.concatenate(parts, axis=0).astype(jnp.bfloat16)
        out_ref[i] = lax.dot_general(
            left, table_ref[...], (((0,), (0,)), ((), ())), preferred_element_type=jnp.float32
        )


def call(kernel, out_shape, dtype, scratch, flops, *args):
    return pl.pallas_call(
        kernel,
        out_shape=jax.ShapeDtypeStruct(out_shape, dtype),
        in_specs=[pl.BlockSpec(memory_space=pltpu.VMEM)] * len(args),
        out_specs=pl.BlockSpec(memory_space=pltpu.VMEM),
        scratch_shapes=scratch,
        compiler_params=pltpu.CompilerParams(vmem_limit_bytes=VMEM),
        cost_estimate=pl.CostEstimate(flops=flops, bytes_accessed=2 << 20, transcendentals=0),
    )(*args)


def shards(recordings, good_windows, response):
    blocks = lax.axis_size("chan")
    core = lax.rem(lax.axis_index("chan"), 2)
    x = recordings.reshape(CB * W, S)
    good = jnp.transpose(good_windows, (0, 2, 1)).reshape(W, CB)
    spectra = call(
        spectra_kernel, (DAYS, W, FS, 2 * CB), jnp.bfloat16,
        [pltpu.VMEM((S // 128, CB * W, 128), jnp.float32), pltpu.VMEM((CB * W, S), jnp.bfloat16)],
        2 * CB * W * S * 2 * F, x, good, response.reshape(1, F), jnp.asarray(dft_table()),
    )
    mine = lax.all_to_all(spectra, "day", 0, 0, tiled=True)
    two = lax.ppermute(mine, "chan", [(b, (b - 2) % blocks) for b in range(blocks)])
    give = jnp.where(core == 0, two, mine)
    one = lax.ppermute(give, "chan", [(b, b ^ 1) for b in range(blocks)])
    cross = call(
        cross_kernel, (DAYS, FS, 16, 2 * CB), jnp.bfloat16,
        [pltpu.VMEM((3, DAYS * W * FS, 2 * CB), jnp.float32)],
        2 * FS * 128 * 128 * 128,
        *(v.reshape(DAYS * W * FS, 2 * CB) for v in (mine, one, two)),
    )
    cross = lax.all_to_all(cross, "day", 0, 0, tiled=True)
    lags = call(
        lag_kernel, (8, 2 * CB, L), jnp.float32,
        [pltpu.VMEM((F * 16, 2 * CB), jnp.float32)],
        2 * 8 * 128 * 512 * 128,
        cross.reshape(F * 16, 2 * CB), jnp.asarray(lag_table()),
    )
    return lags.reshape(8, 2, CB, L)


def solution(mesh):
    in_specs = (P("day", "chan", None, None), P("day", "chan", None), P())
    out_specs = P(("chan", "day"), None, None, None)
    return jax.shard_map(shards, mesh=mesh, in_specs=in_specs, out_specs=out_specs, check_vma=False)
```

time: 231 us -> 84.5 us (0.37)
  the two profiles are of different devices: /device:TPU:1 before, /device:TPU:24 now
where the time goes in v1:
time: 84.5 us; the launch traced here: 84.1 us
  blocking collectives  34.9 us (41%)
  waiting for transfers between devices  27.7 us (33%)
  starting transfers between devices  11.8 us (14%)
  Pallas kernels  6.46 us (8%)
  local copies, waits for them, and re-layouts  3.15 us (4%)
    ppermute x1, waiting for transfers between devices, shards(): lax.ppermute(mine, 'chan', [(b, (b - 2) % blocks) for b in range(blocks)])  25.8 us
    all_to_all x1, blocking collectives, shards(): cross = lax.all_to_all(cross, 'day', 0, 0, tiled=True)  18.8 us
    all_to_all x1, blocking collectives, shards(): mine = lax.all_to_all(spectra, 'day', 0, 0, tiled=True)  16 us
    ppermute x1, starting transfers between devices, shards(): lax.ppermute(mine, 'chan', [(b, (b - 2) % blocks) for b in range(blocks)])  9.91 us
    pallas_call x3, Pallas kernels, call(): pl.pallas_call(kernel, out_shape=jax.ShapeDtypeStruct(out_shape, dtype),...  6.46 us
    unnamed x10, local copies, waits for them, and re-layouts  3.15 us
    ppermute x1, starting transfers between devices, shards(): one = lax.ppermute(give, 'chan', [(b, b ^ 1) for b in range(blocks)])  1.92 us
    ppermute x1, waiting for transfers between devices, shards(): one = lax.ppermute(give, 'chan', [(b, b ^ 1) for b in range(blocks)])  1.88 us
  transfers between devices with their start and end apart: 2, of which 2 were waited for; matrix products, arithmetic and copies ran while one was open for 0% of the time, Pallas kernels for 0%

profile of v1, /device:TPU:24, one launch (start us, length us, event | category | flops | bytes accessed | tf_op | source)
XLA Modules:
  0.0 84.1 jit_solution(824889709142411479)
XLA Ops:
  0.0 0.0 copy-start.3
  0.0 0.0 copy-start.4
  0.0 0.7 copy-done.3
  0.7 0.0 copy-done.4
  0.7 0.0 copy-start
  0.7 1.2 %copy-done = bf16[1,64,8,1024]{3,2,1,0:T(8,128)(2,1)S(1)} copy-done((bf16[1,64,8,1024]{3,2,1,0:T(8,128)(2,1)S(1)}, bf16[1,64,8,1024]{3,2,1,0:T(8,128)(2,1)}, u32[]{:S(2)}) %copy-start) | copy-done | bytes 1048600
  1.9 0.0 copy-start.1
  1.9 1.2 %copy-done.1 = bf16[512,1024]{1,0:T(8,128)(2,1)S(1)} copy-done((bf16[512,1024]{1,0:T(8,128)(2,1)S(1)}, bf16[512,1024]{1,0:T(8,128)(2,1)}, u32[]{:S(2)}) %copy-start.1) | copy-done | bytes 1048600
  3.1 1.4 %shard_map.55 = bf16[8,8,32,128]{3,2,1,0:T(8,128)(2,1)S(1)} custom-call(bf16[512,1024]{1,0:T(8,128)(2,1)S(1)} %bitcast.13, s32[8,64]{1,0:T(8,128)S(1)} %bitcast.15, f32[1,256]{1,0:T(1,128)S(1)} %bitcast.16, bf16[512,1024]{1,0:T(8,128)(2,1)S(1)} %copy-done.1), custom_call_target="tpu_custom_call" | custom-call | flops 536870912 | bytes 2097152 | tf_op jit(solution)/shard_map/pallas_call | solution.py:112
  4.5 16.0 %all_to_all.10 = bf16[8,8,32,128]{3,2,1,0:T(8,128)(2,1)S(1)} all-to-all(bf16[8,8,32,128]{3,2,1,0:T(8,128)(2,1)S(1)} %shard_map.55), channel_id=1, replica_groups=mesh['chan'=64,'day'=8] {'day'}, dimensions={0} | all-to-all | bytes 1048576 | tf_op jit(solution)/shard_map/all_to_all | solution.py:133
  20.6 9.9 %collective-permute-start = (bf16[8,8,32,128]{3,2,1,0:T(8,128)(2,1)S(1)}, bf16[8,8,32,128]{3,2,1,0:T(8,128)(2,1)S(1)}, u32[]{:S(2)}, u32[]{:S(2)}) collective-permute-start(bf16[8,8,32,128]{3,2,1,0:T(8,128)(2,1)S(1)} %all_to_all.10), channel_id=1, source_target_pairs={{0,496},{8,504},{16,0},{24,8},{32,16},{40,24},{48,32},{56,40},{64,... | collective-permute-start | bytes 1572872 | tf_op jit(solution)/shard_map/ppermute | solution.py:134
  30.5 25.8 %collective-permute-done = bf16[8,8,32,128]{3,2,1,0:T(8,128)(2,1)S(1)} collective-permute-done((bf16[8,8,32,128]{3,2,1,0:T(8,128)(2,1)S(1)}, bf16[8,8,32,128]{3,2,1,0:T(8,128)(2,1)S(1)}, u32[]{:S(2)}, u32[]{:S(2)}) %collective-permute-start) | collective-permute-done | bytes 524320 | tf_op jit(solution)/shard_map/ppermute | solution.py:134
  56.3 0.1 broadcast_select_fusion
  56.4 1.9 %collective-permute-start.1 = (bf16[8,8,32,128]{3,2,1,0:T(8,128)(2,1)S(1)}, bf16[8,8,32,128]{3,2,1,0:T(8,128)(2,1)S(1)}, u32[]{:S(2)}, u32[]{:S(2)}) collective-permute-start(bf16[8,8,32,128]{3,2,1,0:T(8,128)(2,1)S(1)} %broadcast_select_fusion), channel_id=1, source_target_pairs={{0,8},{8,0},{16,24},{24,16},{32,40},{40,32},{48,56},{56,48},{64,72... | collective-permute-start | bytes 1572872 | tf_op jit(solution)/shard_map/ppermute | solution.py:136
  58.3 1.9 %collective-permute-done.1 = bf16[8,8,32,128]{3,2,1,0:T(8,128)(2,1)S(1)} collective-permute-done((bf16[8,8,32,128]{3,2,1,0:T(8,128)(2,1)S(1)}, bf16[8,8,32,128]{3,2,1,0:T(8,128)(2,1)S(1)}, u32[]{:S(2)}, u32[]{:S(2)}) %collective-permute-start.1) | collective-permute-done | bytes 524320 | tf_op jit(solution)/shard_map/ppermute | solution.py:136
  60.2 3.2 %shard_map.56 = bf16[8,32,16,128]{3,2,1,0:T(8,128)(2,1)S(1)} custom-call(bf16[2048,128]{1,0:T(8,128)(2,1)S(1)} %bitcast.10, bf16[2048,128]{1,0:T(8,128)(2,1)S(1)} %bitcast.14, bf16[2048,128]{1,0:T(8,128)(2,1)S(1)} %bitcast.12), custom_call_target="tpu_custom_call" | custom-call | flops 134217728 | bytes 2097152 | tf_op jit(solution)/shard_map/pallas_call | solution.py:112
  63.4 0.0 copy-start.2
  63.4 18.8 %all_to_all.11 = bf16[8,32,16,128]{3,2,1,0:T(8,128)(2,1)S(1)} all-to-all(bf16[8,32,16,128]{3,2,1,0:T(8,128)(2,1)S(1)} %shard_map.56), channel_id=1, replica_groups=mesh['chan'=64,'day'=8] {'day'}, dimensions={0} | all-to-all | bytes 2097152 | tf_op jit(solution)/shard_map/all_to_all | solution.py:143
  82.3 0.0 copy-done.2
  82.3 1.9 %shard_map.57 = f32[8,128,128]{2,1,0:T(8,128)} custom-call(bf16[4096,128]{1,0:T(8,128)(2,1)S(1)} %bitcast.11, bf16[512,128]{1,0:T(8,128)(2,1)S(1)} %copy-done.2), custom_call_target="tpu_custom_call" | custom-call | flops 134217728 | bytes 2097152 | tf_op jit(solution)/shard_map/pallas_call | solution.py:112
Async XLA Ops:
  0.0 0.7 copy-start.3
  0.0 0.7 copy-start.4
  0.7 1.2 %copy-start = (bf16[1,64,8,1024]{3,2,1,0:T(8,128)(2,1)S(1)}, bf16[1,64,8,1024]{3,2,1,0:T(8,128)(2,1)}, u32[]{:S(2)}) copy-start(bf16[1,64,8,1024]{3,2,1,0:T(8,128)(2,1)} %param.5) | copy-start | bytes 3145732
  1.9 1.2 %copy-start.1 = (bf16[512,1024]{1,0:T(8,128)(2,1)S(1)}, bf16[512,1024]{1,0:T(8,128)(2,1)}, u32[]{:S(2)}) copy-start(bf16[512,1024]{1,0:T(8,128)(2,1)} %constant.16.clone.table_ref) | copy-start | bytes 3145732
  20.6 35.8 %collective-permute-start = (bf16[8,8,32,128]{3,2,1,0:T(8,128)(2,1)S(1)}, bf16[8,8,32,128]{3,2,1,0:T(8,128)(2,1)S(1)}, u32[]{:S(2)}, u32[]{:S(2)}) collective-permute-start(bf16[8,8,32,128]{3,2,1,0:T(8,128)(2,1)S(1)} %all_to_all.10), channel_id=1, source_target_pairs={{0,496},{8,504},{16,0},{24,8},{32,16},{40,24},{48,32},{56,40},{64,... | collective-permute-start | bytes 1572872 | tf_op jit(solution)/shard_map/ppermute | solution.py:134
  56.4 3.8 %collective-permute-start.1 = (bf16[8,8,32,128]{3,2,1,0:T(8,128)(2,1)S(1)}, bf16[8,8,32,128]{3,2,1,0:T(8,128)(2,1)S(1)}, u32[]{:S(2)}, u32[]{:S(2)}) collective-permute-start(bf16[8,8,32,128]{3,2,1,0:T(8,128)(2,1)S(1)} %broadcast_select_fusion), channel_id=1, source_target_pairs={{0,8},{8,0},{16,24},{24,16},{32,40},{40,32},{48,56},{56,48},{64,72... | collective-permute-start | bytes 1572872 | tf_op jit(solution)/shard_map/ppermute | solution.py:136
  63.4 18.9 %copy-start.2 = (bf16[512,128]{1,0:T(8,128)(2,1)S(1)}, bf16[512,128]{1,0:T(8,128)(2,1)}, u32[]{:S(2)}) copy-start(bf16[512,128]{1,0:T(8,128)(2,1)} %constant.17.clone.table_ref) | copy-start | bytes 393220

commit v2 on v1

v2 whole, which is shorter than its diff:
```python
import math

import jax
import jax.numpy as jnp
import ml_dtypes
import numpy as np
from jax import lax
from jax.experimental import pallas as pl
from jax.experimental.pallas import tpu as pltpu
from jax.sharding import PartitionSpec as P

FIRST_BIN = 4
S = 1024
F = 256
L = 128
CB = 64
W = 8
DAYS = 8
FS = F // DAYS
ROWS = DAYS * W * FS
VMEM = 40 * 1024 * 1024


def phase_table(product):
    phase = np.mod(product, S).astype(np.float32) * np.float32(2.0 * math.pi / S)
    return np.concatenate([np.cos(phase), -np.sin(phase)], axis=0).astype(ml_dtypes.bfloat16)


def dft_table():
    return phase_table((np.arange(F) + FIRST_BIN)[:, None] * np.arange(S)[None, :])


def lag_table():
    return phase_table((np.arange(F) + FIRST_BIN)[:, None] * (np.arange(L) - L // 2)[None, :])


def low_lanes(rows):
    return lax.broadcasted_iota(jnp.int32, (rows, 2 * CB), 1) < CB


def turn(v):
    return pltpu.roll(v, CB, 1)


def spectra_kernel(x_ref, good_ref, resp_ref, table_ref, out_ref, xs, normed):
    lanes = S // 128
    for lane in range(lanes):
        xs[lane] = x_ref[:, 128 * lane : 128 * (lane + 1)].astype(jnp.float32)
    for w in range(W):
        rows = pl.ds(w, CB, stride=W)
        v = jnp.concatenate([xs[lane, rows, :] for lane in range(lanes)], axis=1)
        power = jnp.mean(v * v, axis=-1, keepdims=True)
        normed[pl.ds(w * CB, CB), :] = (v * lax.rsqrt(power + 1e-06)).astype(jnp.bfloat16)
    gain = jnp.transpose(jnp.broadcast_to(resp_ref[...], (2 * CB, F)))
    low = low_lanes(F)
    good = good_ref[...].astype(jnp.float32)
    for half in range(2):
        rows = normed[pl.ds(half * 4 * CB, 4 * CB), :]
        spectra = lax.dot_general(
            table_ref[...], rows, (((1,), (1,)), ((), ())), preferred_element_type=jnp.float32
        )
        for pair in range(2):
            w = 4 * half + 2 * pair
            mask = jnp.concatenate([good[w : w + 1, :], good[w + 1 : w + 2, :]], axis=1)
            weight = gain * mask
            cols = slice(2 * CB * pair, 2 * CB * (pair + 1))
            re = spectra[:F, cols] * weight
            im = spectra[F:, cols] * weight
            first = jnp.where(low, re, turn(im)).astype(jnp.bfloat16).reshape(DAYS, FS, 2 * CB)
            second = jnp.where(low, turn(re), im).astype(jnp.bfloat16).reshape(DAYS, FS, 2 * CB)
            for to in range(2):
                out_ref[to, :, w] = first
                out_ref[to, :, w + 1] = second


def cross_into(out_ref, left, right):
    low = low_lanes(DAYS * W)
    for pair in range(FS // 2):
        both = []
        for f in (2 * pair, 2 * pair + 1):
            rows = pl.ds(f, DAYS * W, stride=FS)
            one, two = left[rows, :], right[rows, :]
            lhs = jnp.concatenate([one, turn(one)], axis=0)[:, :CB].astype(jnp.bfloat16)
            rhs = jnp.concatenate([jnp.where(low, two, -two), turn(two)], axis=0).astype(jnp.bfloat16)
            both.append(
                lax.dot_general(lhs, rhs, (((0,), (0,)), ((), ())), preferred_element_type=jnp.float32)
            )
        for k in range(DAYS):
            piece = jnp.concatenate([v[8 * k : 8 * k + 8] for v in both], axis=0)
            out_ref[k, pl.ds(16 * pair, 16), :] = piece.astype(jnp.bfloat16)


def second_kernel(odd_ref, near_ref, swap_ref, out_ref, left, right):
    odd = odd_ref[0] == 1

    @pl.when(odd)
    def _():
        left[...] = swap_ref[...].astype(jnp.float32)
        right[...] = near_ref[1].astype(jnp.float32)

    @pl.when(jnp.logical_not(odd))
    def _():
        left[...] = near_ref[0].astype(jnp.float32)
        right[...] = swap_ref[...].astype(jnp.float32)

    cross_into(out_ref, left, right)


def first_kernel(odd_ref, near_ref, swap_ref, out_ref, left, right):
    odd = odd_ref[0] == 1

    @pl.when(odd)
    def _():
        left[...] = near_ref[0].astype(jnp.float32)
        right[...] = near_ref[1].astype(jnp.float32)

    @pl.when(jnp.logical_not(odd))
    def _():
        left[...] = near_ref[1].astype(jnp.float32)
        right[...] = swap_ref[...].astype(jnp.float32)

    cross_into(out_ref, left, right)


def lags_of(cross_ref, table_ref, wide):
    wide[...] = cross_ref[...].astype(jnp.float32)
    low = low_lanes(F)
    for pair in range(4):
        one, two = (wide[pl.ds(2 * pair + i, F, stride=8), :] for i in range(2))
        re = jnp.where(low, one, turn(two))
        im = jnp.where(low, turn(one), two)
        yield pair, lax.dot_general(
            jnp.concatenate([re, im], axis=0).astype(jnp.bfloat16), table_ref[...],
            (((0,), (0,)), ((), ())), preferred_element_type=jnp.float32,
        ).reshape(2, CB, L)


def second_lag_kernel(cross_ref, table_ref, out_ref, wide):
    for pair, lags in lags_of(cross_ref, table_ref, wide):
        out_ref[pl.ds(2 * pair, 2)] = lags.astype(jnp.bfloat16)


def first_lag_kernel(cross_ref, table_ref, second_ref, out_ref, wide):
    for pair, lags in lags_of(cross_ref, table_ref, wide):
        out_ref[pl.ds(2 * pair, 2), 0] = lags
    out_ref[:, 1] = second_ref[...].astype(jnp.float32)


def call(kernel, out_shape, dtype, scratch, flops, *args, scalars=0):
    smem = [pl.BlockSpec(memory_space=pltpu.SMEM)] * scalars
    return pl.pallas_call(
        kernel,
        out_shape=jax.ShapeDtypeStruct(out_shape, dtype),
        in_specs=smem + [pl.BlockSpec(memory_space=pltpu.VMEM)] * (len(args) - scalars),
        out_specs=pl.BlockSpec(memory_space=pltpu.VMEM),
        scratch_shapes=scratch,
        compiler_params=pltpu.CompilerParams(vmem_limit_bytes=VMEM),
        cost_estimate=pl.CostEstimate(flops=flops, bytes_accessed=2 << 20, transcendentals=0),
    )(*args)


WIDE = pltpu.VMEM((ROWS, 2 * CB), jnp.float32)
CROSS_FLOPS = 2 * FS * 64 * 128 * 128
LAG_FLOPS = 2 * 8 * 64 * 512 * 128
CROSS_SHAPE = (DAYS, FS * 8, 2 * CB)


def spectra_call(x, good, response):
    return call(
        spectra_kernel, (2, DAYS, W, FS, 2 * CB), jnp.bfloat16,
        [pltpu.VMEM((S // 128, CB * W, 128), jnp.float32), pltpu.VMEM((CB * W, S), jnp.bfloat16)],
        2 * CB * W * S * 2 * F, x, good, response, jnp.asarray(dft_table()),
    )


def second_call(flag, near, swap):
    return call(second_kernel, CROSS_SHAPE, jnp.bfloat16, [WIDE, WIDE], CROSS_FLOPS, flag, near, swap, scalars=1)


def first_call(flag, near, swap):
    return call(first_kernel, CROSS_SHAPE, jnp.bfloat16, [WIDE, WIDE], CROSS_FLOPS, flag, near, swap, scalars=1)


def second_lag_call(cross):
    return call(second_lag_kernel, (8, CB, L), jnp.bfloat16, [WIDE], LAG_FLOPS, cross, jnp.asarray(lag_table()))


def first_lag_call(cross, second):
    return call(
        first_lag_kernel, (8, 2, CB, L), jnp.float32, [WIDE], LAG_FLOPS, cross, jnp.asarray(lag_table()), second
    )


def shards(recordings, good_windows, response):
    blocks = lax.axis_size("chan")
    odd = lax.rem(lax.axis_index("chan"), 2)
    flag = odd.astype(jnp.int32).reshape(1)
    x = recordings.reshape(CB * W, S)
    good = jnp.transpose(good_windows, (0, 2, 1)).reshape(W, CB)
    spectra = spectra_call(x, good, response.reshape(1, F))
    groups = [
        [b % blocks * DAYS + d for b in (block, block + 1) for d in range(DAYS)]
        for block in range(1, blocks, 2)
    ]
    near = lax.all_to_all(
        spectra.reshape(2 * DAYS, W, FS, 2 * CB), ("chan", "day"), 0, 0, axis_index_groups=groups, tiled=True
    ).reshape(2, ROWS, 2 * CB)
    mine = jnp.where(odd == 1, near[0], near[1])
    swap = lax.ppermute(mine, "chan", [(b, b ^ 1) for b in range(blocks)])
    second = lax.all_to_all(second_call(flag, near, swap), "day", 0, 0, tiled=True)
    first = lax.all_to_all(first_call(flag, near, swap), "day", 0, 0, tiled=True)
    second = second_lag_call(second.reshape(F * 8, 2 * CB))
    second = lax.ppermute(second, "chan", [(b, (b - 1) % blocks) for b in range(blocks)])
    return first_lag_call(first.reshape(F * 8, 2 * CB), second)


def solution(mesh):
    in_specs = (P("day", "chan", None, None), P("day", "chan", None), P())
    out_specs = P(("chan", "day"), None, None, None)
    return jax.shard_map(shards, mesh=mesh, in_specs=in_specs, out_specs=out_specs, check_vma=False)
```

time: 84.5 us -> 75.9 us (0.90)
  the two profiles are of different devices: /device:TPU:24 before, /device:TPU:2 now
where the time goes in v2:
time: 75.9 us; the launch traced here: 75.4 us
  starting transfers between devices  36.9 us (49%)
  waiting for transfers between devices  24.5 us (32%)
  Pallas kernels  10.8 us (14%)
  local copies, waits for them, and re-layouts  3.15 us (4%)
    all_to_all x1, starting transfers between devices, shards(): lax.all_to_all(spectra.reshape(2 * DAYS, W, FS, 2 * CB), ('chan', 'day'),...  16.3 us
    all_to_all x1, waiting for transfers between devices, shards(): lax.all_to_all(spectra.reshape(2 * DAYS, W, FS, 2 * CB), ('chan', 'day'),...  14.7 us
    pallas_call x5, Pallas kernels, call(): pl.pallas_call(kernel, out_shape=jax.ShapeDtypeStruct(out_shape, dtype),...  10.8 us
    ppermute x1, starting transfers between devices, shards(): lax.ppermute(second, 'chan', [(b, (b - 1) % blocks) for b in range(blocks)])  8.33 us
    all_to_all x1, waiting for transfers between devices, shards(): lax.all_to_all(second_call(flag, near, swap), 'day', 0, 0, tiled=True)  5.5 us
    all_to_all x1, starting transfers between devices, shards(): lax.all_to_all(first_call(flag, near, swap), 'day', 0, 0, tiled=True)  5.42 us
    all_to_all x1, starting transfers between devices, shards(): lax.all_to_all(second_call(flag, near, swap), 'day', 0, 0, tiled=True)  4.91 us
    unnamed x10, local copies, waits for them, and re-layouts  3.15 us
  transfers between devices with their start and end apart: 5, of which 4 were waited for; matrix products, arithmetic and copies ran while one was open for 0% of the time, Pallas kernels for 5%

profile of v2, /device:TPU:2, one launch (start us, length us, event | category | flops | bytes accessed | tf_op | source)
XLA Modules:
  0.0 75.4 jit_solution(1479838129800194265)
XLA Ops:
  0.0 0.0 copy-start.3
  0.0 0.0 copy-start.4
  0.0 0.7 copy-done.3
  0.7 0.0 copy-done.4
  0.7 0.0 copy-start
  0.7 1.2 %copy-done = bf16[1,64,8,1024]{3,2,1,0:T(8,128)(2,1)S(1)} copy-done((bf16[1,64,8,1024]{3,2,1,0:T(8,128)(2,1)S(1)}, bf16[1,64,8,1024]{3,2,1,0:T(8,128)(2,1)}, u32[]{:S(2)}) %copy-start) | copy-done | bytes 1048600
  1.9 0.0 copy-start.1
  1.9 1.2 %copy-done.1 = bf16[512,1024]{1,0:T(8,128)(2,1)S(1)} copy-done((bf16[512,1024]{1,0:T(8,128)(2,1)S(1)}, bf16[512,1024]{1,0:T(8,128)(2,1)}, u32[]{:S(2)}) %copy-start.1) | copy-done | bytes 1048600
  3.1 2.4 %shard_map.64 = bf16[2,8,8,32,128]{4,3,2,1,0:T(8,128)(2,1)} custom-call(bf16[512,1024]{1,0:T(8,128)(2,1)S(1)} %bitcast.15, s32[8,64]{1,0:T(8,128)S(1)} %bitcast.16, f32[1,256]{1,0:T(1,128)S(1)} %bitcast.17, bf16[512,1024]{1,0:T(8,128)(2,1)S(1)} %copy-done.1), custom_call_target="tpu_custom_call" | custom-call | flops 536870912 | bytes 2097152 | tf_op jit(solution)/shard_map/pallas_call | solution.py:151
  5.5 16.3 %all-to-all-start = ((bf16[16,8,32,128]{3,2,1,0:T(8,128)(2,1)}), bf16[16,8,32,128]{3,2,1,0:T(8,128)(2,1)S(1)}, u32[]{:S(2)}, u32[]{:S(2)}) async-start(bf16[16,8,32,128]{3,2,1,0:T(8,128)(2,1)} %bitcast.5), calls=%async_computation | async-start | bytes 2097152 | tf_op jit(solution)/shard_map/all_to_all | solution.py:205
  21.8 14.7 %all-to-all-done = bf16[16,8,32,128]{3,2,1,0:T(8,128)(2,1)S(1)} async-done(((bf16[16,8,32,128]{3,2,1,0:T(8,128)(2,1)}), bf16[16,8,32,128]{3,2,1,0:T(8,128)(2,1)S(1)}, u32[]{:S(2)}, u32[]{:S(2)}) %all-to-all-start) | async-done | bytes 1048608 | tf_op jit(solution)/shard_map/all_to_all | solution.py:205
  36.5 0.1 slice_select_fusion
  36.5 1.9 %collective-permute-start = (bf16[2048,128]{1,0:T(8,128)(2,1)S(1)}, bf16[2048,128]{1,0:T(8,128)(2,1)S(1)}, u32[]{:S(2)}, u32[]{:S(2)}) collective-permute-start(bf16[2048,128]{1,0:T(8,128)(2,1)S(1)} %bitcast.18), channel_id=1, source_target_pairs={{0,8},{8,0},{16,24},{24,16},{32,40},{40,32},{48,56},{56,48},{64,72... | collective-permute-start | bytes 1572872 | tf_op jit(solution)/shard_map/ppermute | solution.py:209
  38.5 1.9 %collective-permute-done.swap_ref = bf16[2048,128]{1,0:T(8,128)(2,1)S(1)} collective-permute-done((bf16[2048,128]{1,0:T(8,128)(2,1)S(1)}, bf16[2048,128]{1,0:T(8,128)(2,1)S(1)}, u32[]{:S(2)}, u32[]{:S(2)}) %collective-permute-start) | collective-permute-done | bytes 524320 | tf_op jit(solution)/shard_map/ppermute | solution.py:209
  40.3 3.1 %shard_map.66 = bf16[8,256,128]{2,1,0:T(8,128)(2,1)} custom-call(s32[1]{0:T(128)} %bitcast.odd_ref, bf16[2,2048,128]{2,1,0:T(8,128)(2,1)S(1)} %bitcast.11, bf16[2048,128]{1,0:T(8,128)(2,1)S(1)} %collective-permute-done.swap_ref), custom_call_target="tpu_custom_call" | custom-call | flops 67108864 | bytes 2097152 | tf_op jit(solution)/shard_map/pallas_call | solution.py:151
  43.4 4.9 %all-to-all-start.2 = ((bf16[8,256,128]{2,1,0:T(8,128)(2,1)}), bf16[8,256,128]{2,1,0:T(8,128)(2,1)S(1)}, u32[]{:S(2)}, u32[]{:S(2)}) async-start(bf16[8,256,128]{2,1,0:T(8,128)(2,1)} %shard_map.66), calls=%async_computation.2 | async-start | bytes 1048576 | tf_op jit(solution)/shard_map/all_to_all | solution.py:210
  48.3 3.1 %shard_map.65 = bf16[8,256,128]{2,1,0:T(8,128)(2,1)} custom-call(s32[1]{0:T(128)} %bitcast.odd_ref, bf16[2,2048,128]{2,1,0:T(8,128)(2,1)S(1)} %bitcast.12, bf16[2048,128]{1,0:T(8,128)(2,1)S(1)} %collective-permute-done.swap_ref), custom_call_target="tpu_custom_call" | custom-call | flops 67108864 | bytes 2097152 | tf_op jit(solution)/shard_map/pallas_call | solution.py:151
  51.4 0.0 copy-start.2
  51.4 5.5 %all-to-all-done.2 = bf16[8,256,128]{2,1,0:T(8,128)(2,1)S(1)} async-done(((bf16[8,256,128]{2,1,0:T(8,128)(2,1)}), bf16[8,256,128]{2,1,0:T(8,128)(2,1)S(1)}, u32[]{:S(2)}, u32[]{:S(2)}) %all-to-all-start.2) | async-done | bytes 524320 | tf_op jit(solution)/shard_map/all_to_all | solution.py:210
  56.9 5.4 %all-to-all-start.1 = ((bf16[8,256,128]{2,1,0:T(8,128)(2,1)}), bf16[8,256,128]{2,1,0:T(8,128)(2,1)S(1)}, u32[]{:S(2)}, u32[]{:S(2)}) async-start(bf16[8,256,128]{2,1,0:T(8,128)(2,1)} %shard_map.65), calls=%async_computation.1 | async-start | bytes 1048576 | tf_op jit(solution)/shard_map/all_to_all | solution.py:211
  62.4 0.0 copy-done.2
  62.4 0.7 shard_map.67
  63.1 8.3 %collective-permute-start.1 = (bf16[8,64,128]{2,1,0:T(8,128)(2,1)S(1)}, bf16[8,64,128]{2,1,0:T(8,128)(2,1)S(1)}, u32[]{:S(2)}, u32[]{:S(2)}) collective-permute-start(bf16[8,64,128]{2,1,0:T(8,128)(2,1)S(1)} %shard_map.67), channel_id=1, source_target_pairs={{0,504},{8,0},{16,8},{24,16},{32,24},{40,32},{48,40},{56,48},{64,5... | collective-permute-start | bytes 393224 | tf_op jit(solution)/shard_map/ppermute | solution.py:213
  71.4 0.0 all-to-all-done.1
  71.4 2.5 %collective-permute-done.1.second_ref = bf16[8,64,128]{2,1,0:T(8,128)(2,1)S(1)} collective-permute-done((bf16[8,64,128]{2,1,0:T(8,128)(2,1)S(1)}, bf16[8,64,128]{2,1,0:T(8,128)(2,1)S(1)}, u32[]{:S(2)}, u32[]{:S(2)}) %collective-permute-start.1) | collective-permute-done | bytes 131104 | tf_op jit(solution)/shard_map/ppermute | solution.py:213
  73.9 1.5 %shard_map.68 = f32[8,2,64,128]{3,2,1,0:T(8,128)} custom-call(bf16[2048,128]{1,0:T(8,128)(2,1)S(1)} %bitcast.13, bf16[512,128]{1,0:T(8,128)(2,1)S(1)} %copy-done.2, bf16[8,64,128]{2,1,0:T(8,128)(2,1)S(1)} %collective-permute-done.1.second_ref), custom_call_target="tpu_custom_call" | custom-call | flops 67108864 | bytes 2097152 | tf_op jit(solution)/shard_map/pallas_call | solution.py:151
Async XLA Ops:
  0.0 0.7 copy-start.3
  0.0 0.7 copy-start.4
  0.7 1.2 %copy-start = (bf16[1,64,8,1024]{3,2,1,0:T(8,128)(2,1)S(1)}, bf16[1,64,8,1024]{3,2,1,0:T(8,128)(2,1)}, u32[]{:S(2)}) copy-start(bf16[1,64,8,1024]{3,2,1,0:T(8,128)(2,1)} %param.6) | copy-start | bytes 3145732
  1.9 1.2 %copy-start.1 = (bf16[512,1024]{1,0:T(8,128)(2,1)S(1)}, bf16[512,1024]{1,0:T(8,128)(2,1)}, u32[]{:S(2)}) copy-start(bf16[512,1024]{1,0:T(8,128)(2,1)} %constant.16.clone.table_ref) | copy-start | bytes 3145732
  5.5 31.0 %all-to-all-start = ((bf16[16,8,32,128]{3,2,1,0:T(8,128)(2,1)}), bf16[16,8,32,128]{3,2,1,0:T(8,128)(2,1)S(1)}, u32[]{:S(2)}, u32[]{:S(2)}) async-start(bf16[16,8,32,128]{3,2,1,0:T(8,128)(2,1)} %bitcast.5), calls=%async_computation | async-start | bytes 2097152 | tf_op jit(solution)/shard_map/all_to_all | solution.py:205
  36.5 3.8 %collective-permute-start = (bf16[2048,128]{1,0:T(8,128)(2,1)S(1)}, bf16[2048,128]{1,0:T(8,128)(2,1)S(1)}, u32[]{:S(2)}, u32[]{:S(2)}) collective-permute-start(bf16[2048,128]{1,0:T(8,128)(2,1)S(1)} %bitcast.18), channel_id=1, source_target_pairs={{0,8},{8,0},{16,24},{24,16},{32,40},{40,32},{48,56},{56,48},{64,72... | collective-permute-start | bytes 1572872 | tf_op jit(solution)/shard_map/ppermute | solution.py:209
  43.4 13.5 %all-to-all-start.2 = ((bf16[8,256,128]{2,1,0:T(8,128)(2,1)}), bf16[8,256,128]{2,1,0:T(8,128)(2,1)S(1)}, u32[]{:S(2)}, u32[]{:S(2)}) async-start(bf16[8,256,128]{2,1,0:T(8,128)(2,1)} %shard_map.66), calls=%async_computation.2 | async-start | bytes 1048576 | tf_op jit(solution)/shard_map/all_to_all | solution.py:210
  51.4 10.9 %copy-start.2 = (bf16[512,128]{1,0:T(8,128)(2,1)S(1)}, bf16[512,128]{1,0:T(8,128)(2,1)}, u32[]{:S(2)}) copy-start(bf16[512,128]{1,0:T(8,128)(2,1)} %constant.17.clone.table_ref) | copy-start | bytes 393220
  56.9 14.5 %all-to-all-start.1 = ((bf16[8,256,128]{2,1,0:T(8,128)(2,1)}), bf16[8,256,128]{2,1,0:T(8,128)(2,1)S(1)}, u32[]{:S(2)}, u32[]{:S(2)}) async-start(bf16[8,256,128]{2,1,0:T(8,128)(2,1)} %shard_map.65), calls=%async_computation.1 | async-start | bytes 1048576 | tf_op jit(solution)/shard_map/all_to_all | solution.py:211
  63.1 10.8 %collective-permute-start.1 = (bf16[8,64,128]{2,1,0:T(8,128)(2,1)S(1)}, bf16[8,64,128]{2,1,0:T(8,128)(2,1)S(1)}, u32[]{:S(2)}, u32[]{:S(2)}) collective-permute-start(bf16[8,64,128]{2,1,0:T(8,128)(2,1)S(1)} %shard_map.67), channel_id=1, source_target_pairs={{0,504},{8,0},{16,8},{24,16},{32,24},{40,32},{48,40},{56,48},{64,5... | collective-permute-start | bytes 393224 | tf_op jit(solution)/shard_map/ppermute | solution.py:213

commit v3 on v2

v3 whole, which is shorter than its diff:
```python
import math

import jax
import jax.numpy as jnp
import ml_dtypes
import numpy as np
from jax import lax
from jax.experimental import pallas as pl
from jax.experimental.pallas import tpu as pltpu
from jax.sharding import PartitionSpec as P

FIRST_BIN = 4
S = 1024
F = 256
L = 128
CB = 64
W = 8
DAYS = 8
FS = F // DAYS
ROWS = DAYS * W * FS
VMEM = 24 * 1024 * 1024
PARTS = 4


def phase_table(product):
    phase = np.mod(product, S).astype(np.float32) * np.float32(2.0 * math.pi / S)
    return np.concatenate([np.cos(phase), -np.sin(phase)], axis=0).astype(ml_dtypes.bfloat16)


def dft_table():
    return phase_table((np.arange(F) + FIRST_BIN)[:, None] * np.arange(S)[None, :])


def lag_table():
    return phase_table((np.arange(F) + FIRST_BIN)[:, None] * (np.arange(L) - L // 2)[None, :])


def low_lanes(rows):
    return lax.broadcasted_iota(jnp.int32, (rows, 2 * CB), 1) < CB


def turn(v):
    return pltpu.roll(v, CB, 1)


def spectra_kernel(x_hbm, good_hbm, resp_hbm, table_hbm, out_ref, x_ref, good_ref, resp_ref, table_ref, xs, normed, sems):
    part = CB // PARTS
    pairs = [(x_hbm.at[pl.ds(p * part * W, part * W)], x_ref.at[pl.ds(p * part * W, part * W)]) for p in range(PARTS)]
    pairs += [(good_hbm, good_ref), (resp_hbm, resp_ref), (table_hbm, table_ref)]
    copies = [pltpu.make_async_copy(source, target, sems.at[at]) for at, (source, target) in enumerate(pairs)]
    for copy in copies:
        copy.start()
    lanes = S // 128
    for p in range(PARTS):
        copies[p].wait()
        rows = pl.ds(p * part * W, part * W)
        for lane in range(lanes):
            xs[lane, rows, :] = x_ref[rows, 128 * lane : 128 * (lane + 1)].astype(jnp.float32)
        for w in range(W):
            rows = pl.ds(p * part * W + w, part, stride=W)
            v = jnp.concatenate([xs[lane, rows, :] for lane in range(lanes)], axis=1)
            power = jnp.mean(v * v, axis=-1, keepdims=True)
            scaled = (v * lax.rsqrt(power + 1e-06)).astype(jnp.bfloat16)
            normed[pl.ds(w * CB + p * part, part), :] = scaled
    for copy in copies[PARTS:]:
        copy.wait()
    gain = jnp.transpose(jnp.broadcast_to(resp_ref[...], (2 * CB, F)))
    low = low_lanes(F)
    good = good_ref[...].astype(jnp.float32)
    for half in range(2):
        rows = normed[pl.ds(half * 4 * CB, 4 * CB), :]
        spectra = lax.dot_general(
            table_ref[...], rows, (((1,), (1,)), ((), ())), preferred_element_type=jnp.float32
        )
        for pair in range(2):
            w = 4 * half + 2 * pair
            mask = jnp.concatenate([good[w : w + 1, :], good[w + 1 : w + 2, :]], axis=1)
            weight = gain * mask
            cols = slice(2 * CB * pair, 2 * CB * (pair + 1))
            re = spectra[:F, cols] * weight
            im = spectra[F:, cols] * weight
            first = jnp.where(low, re, turn(im)).astype(jnp.bfloat16).reshape(DAYS, FS, 2 * CB)
            second = jnp.where(low, turn(re), im).astype(jnp.bfloat16).reshape(DAYS, FS, 2 * CB)
            for to in range(2):
                out_ref[to, :, w] = first
                out_ref[to, :, w + 1] = second


def cross_into(out_ref, left, right):
    low = low_lanes(DAYS * W)
    blank = jnp.zeros((2 * DAYS * W, 2 * CB), jnp.bfloat16)
    for pair in range(FS // 2):
        rows = [pl.ds(2 * pair + f, DAYS * W, stride=FS) for f in range(2)]
        one, other = (left[r, :] for r in rows)
        both = [jnp.where(low, one, turn(other)), jnp.where(low, turn(one), other)]
        both = jnp.transpose(jnp.concatenate(both, axis=0)).astype(jnp.bfloat16)
        parts = []
        for r in rows:
            two = right[r, :]
            parts.append(jnp.concatenate([jnp.where(low, two, -two), turn(two)], axis=0).astype(jnp.bfloat16))
        parts = [jnp.concatenate([parts[0], blank], axis=1), jnp.concatenate([blank, parts[1]], axis=1)]
        cross = jnp.dot(
            jnp.concatenate([both[:CB], both[CB:]], axis=1), jnp.concatenate(parts, axis=0),
            preferred_element_type=jnp.float32,
        )
        for k in range(DAYS):
            rows = slice(8 * k, 8 * k + 8)
            piece = jnp.concatenate([cross[rows, : 2 * CB], cross[rows, 2 * CB :]], axis=0)
            out_ref[k, pl.ds(16 * pair, 16), :] = piece.astype(jnp.bfloat16)


def second_kernel(odd_ref, near_ref, swap_ref, out_ref, left, right):
    @pl.when(odd_ref[0] == 1)
    def _():
        left[...] = swap_ref[...].astype(jnp.float32)
        right[...] = near_ref[1].astype(jnp.float32)

    @pl.when(odd_ref[0] == 0)
    def _():
        left[...] = near_ref[0].astype(jnp.float32)
        right[...] = swap_ref[...].astype(jnp.float32)

    cross_into(out_ref, left, right)


def first_kernel(odd_ref, near_ref, swap_ref, out_ref, left, right):
    @pl.when(odd_ref[0] == 1)
    def _():
        left[...] = near_ref[0].astype(jnp.float32)
        right[...] = near_ref[1].astype(jnp.float32)

    @pl.when(odd_ref[0] == 0)
    def _():
        left[...] = near_ref[1].astype(jnp.float32)
        right[...] = swap_ref[...].astype(jnp.float32)

    cross_into(out_ref, left, right)


def lags_of(wide, table):
    bins = wide.shape[0] // 8
    low = low_lanes(bins)
    for pair in range(4):
        one, two = (wide[pl.ds(2 * pair + i, bins, stride=8), :] for i in range(2))
        re = jnp.where(low, one, turn(two))
        im = jnp.where(low, turn(one), two)
        yield pl.ds(2 * pair, 2), lax.dot_general(
            jnp.concatenate([re, im], axis=0).astype(jnp.bfloat16), table,
            (((0,), (0,)), ((), ())), preferred_element_type=jnp.float32,
        ).reshape(2, CB, L)


def lag_kernel(cross_ref, table_ref, out_ref, wide):
    wide[...] = cross_ref[...].astype(jnp.float32)
    for rows, lags in lags_of(wide, table_ref[...]):
        out_ref[rows] = lags.astype(out_ref.dtype)


def join_kernel(first_ref, second_ref, out_ref):
    out_ref[:, 0] = first_ref[...]
    out_ref[:, 1] = second_ref[...].astype(jnp.float32)


def call(kernel, out_shape, dtype, scratch, flops, *args, scalars=0, space=pltpu.VMEM, limit=VMEM):
    smem = [pl.BlockSpec(memory_space=pltpu.SMEM)] * scalars
    if dtype is not None:
        out_shape = jax.ShapeDtypeStruct(out_shape, dtype)
    return pl.pallas_call(
        kernel,
        out_shape=out_shape,
        in_specs=smem + [pl.BlockSpec(memory_space=space)] * (len(args) - scalars),
        out_specs=jax.tree.map(lambda _: pl.BlockSpec(memory_space=pltpu.VMEM), out_shape),
        scratch_shapes=scratch,
        compiler_params=pltpu.CompilerParams(vmem_limit_bytes=limit),
        cost_estimate=pl.CostEstimate(flops=flops, bytes_accessed=2 << 20, transcendentals=0),
    )(*args)


WHOLE = pltpu.VMEM((ROWS, 2 * CB), jnp.float32)
UNIT_FLOPS = 2 * 64 * 256 * 128
LAG_FLOPS = 2 * 8 * 64 * 512 * 128


def spectra_call(x, good, response):
    operands = (x, good, response, jnp.asarray(dft_table()))
    scratch = [pltpu.VMEM(v.shape, v.dtype) for v in operands]
    scratch += [pltpu.VMEM((S // 128, CB * W, 128), jnp.float32), pltpu.VMEM((CB * W, S), jnp.bfloat16)]
    return call(
        spectra_kernel, (2, DAYS, W, FS, 2 * CB), jnp.bfloat16, scratch + [pltpu.SemaphoreType.DMA((PARTS + 3,))],
        2 * CB * W * S * 2 * F, *operands, space=pltpu.HBM, limit=56 * 1024 * 1024,
    )


def exchange(v):
    return lax.all_to_all(v, "day", 0, 0, tiled=True)


def shards(recordings, good_windows, response):
    blocks = lax.axis_size("chan")
    odd = lax.rem(lax.axis_index("chan"), 2)
    flag = odd.astype(jnp.int32).reshape(1)
    x = recordings.reshape(CB * W, S)
    good = jnp.transpose(good_windows, (0, 2, 1)).reshape(W, CB)
    table = jnp.asarray(lag_table())
    spectra = spectra_call(x, good, response.reshape(1, F))
    groups = [
        [b % blocks * DAYS + d for b in (block, block + 1) for d in range(DAYS)]
        for block in range(1, blocks, 2)
    ]
    near = lax.all_to_all(
        spectra.reshape(2 * DAYS, W, FS, 2 * CB), ("chan", "day"), 0, 0, axis_index_groups=groups, tiled=True
    ).reshape(2, ROWS, 2 * CB)
    mine = jnp.where(odd == 1, near[0], near[1])
    swap = lax.ppermute(mine, "chan", [(b, b ^ 1) for b in range(blocks)])

    def cross(kernel):
        return call(
            kernel, (DAYS, FS * 8, 2 * CB), jnp.bfloat16, [WHOLE] * 2, FS * UNIT_FLOPS, flag, near, swap, scalars=1
        )

    def lags(pairs, dtype):
        return call(
            lag_kernel, (8, CB, L), dtype, [WHOLE], LAG_FLOPS, pairs.reshape(F * 8, 2 * CB), table
        )

    second = exchange(cross(second_kernel))
    first = exchange(cross(first_kernel))
    second = lags(second, jnp.bfloat16)
    second = lax.ppermute(second, "chan", [(b, (b - 1) % blocks) for b in range(blocks)])
    first = lags(first, jnp.float32)
    return call(join_kernel, (8, 2, CB, L), jnp.float32, [], 1 << 17, first, second)


def solution(mesh):
    in_specs = (P("day", "chan", None, None), P("day", "chan", None), P())
    out_specs = P(("chan", "day"), None, None, None)
    return jax.shard_map(shards, mesh=mesh, in_specs=in_specs, out_specs=out_specs, check_vma=False)
```

time: 75.9 us -> 73.1 us (0.963)
  local copies, waits for them, and re-layouts: 3.15 us -> 0.01 us
    unnamed x10 -> x2, local copies, waits for them, and re-layouts: 3.15 us -> 0.01 us
    pallas_call x5 -> x6, Pallas kernels: 10.8 us -> 11.5 us  [call(): pl.pallas_call(kernel, out_shape=out_shape, in_specs=smem + [pl.BlockSpec...]
  transfers between devices with their start and end apart: 5 -> 5, of which waited for: 4 -> 4; matrix products, arithmetic and copies ran while one was open for 0% -> 0% of each run, Pallas kernels for 5% -> 6%
where the time goes in v3:
time: 73.1 us; the launch traced here: 72.7 us
  starting transfers between devices  36.9 us (50%)
  waiting for transfers between devices  24.1 us (33%)
  Pallas kernels  11.5 us (16%)
    all_to_all x1, starting transfers between devices, shards(): lax.all_to_all(spectra.reshape(2 * DAYS, W, FS, 2 * CB), ('chan', 'day'),...  16.3 us
    all_to_all x1, waiting for transfers between devices, shards(): lax.all_to_all(spectra.reshape(2 * DAYS, W, FS, 2 * CB), ('chan', 'day'),...  14.7 us
    pallas_call x6, Pallas kernels, call(): pl.pallas_call(kernel, out_shape=out_shape, in_specs=smem + [pl.BlockSpec...  11.5 us
    all_to_all x2, starting transfers between devices, exchange(): return lax.all_to_all(v, 'day', 0, 0, tiled=True)  10.3 us
    ppermute x1, starting transfers between devices, shards(): lax.ppermute(second, 'chan', [(b, (b - 1) % blocks) for b in range(blocks)])  8.34 us
    all_to_all x2, waiting for transfers between devices, exchange(): return lax.all_to_all(v, 'day', 0, 0, tiled=True)  5.81 us
    ppermute x1, starting transfers between devices, shards(): swap = lax.ppermute(mine, 'chan', [(b, b ^ 1) for b in range(blocks)])  1.92 us
    ppermute x1, waiting for transfers between devices, shards(): swap = lax.ppermute(mine, 'chan', [(b, b ^ 1) for b in range(blocks)])  1.88 us
  transfers between devices with their start and end apart: 5, of which 4 were waited for; matrix products, arithmetic and copies ran while one was open for 0% of the time, Pallas kernels for 6%

profile of v3, /device:TPU:2, one launch (start us, length us, event | category | flops | bytes accessed | tf_op | source)
XLA Modules:
  0.0 72.7 jit_solution(13882335418732707127)
XLA Ops:
  0.0 3.7 %shard_map.55 = bf16[2,8,8,32,128]{4,3,2,1,0:T(8,128)(2,1)} custom-call(bf16[512,1024]{1,0:T(8,128)(2,1)} %bitcast.16, s32[8,64]{1,0:T(8,128)} %bitcast.18, f32[1,256]{1,0:T(1,128)} %bitcast.19, bf16[512,1024]{1,0:T(8,128)(2,1)} %constant.17.clone.table_hbm), custom_call_target="tpu_custom_call" | custom-call | flops 536870912 | bytes 2097152 | tf_op jit(solution)/shard_map/pallas_call | solution.py:168
  3.7 16.3 %all-to-all-start = ((bf16[16,8,32,128]{3,2,1,0:T(8,128)(2,1)}), bf16[16,8,32,128]{3,2,1,0:T(8,128)(2,1)S(1)}, u32[]{:S(2)}, u32[]{:S(2)}) async-start(bf16[16,8,32,128]{3,2,1,0:T(8,128)(2,1)} %bitcast.15), calls=%async_computation | async-start | bytes 2097152 | tf_op jit(solution)/shard_map/all_to_all | solution.py:210
  20.0 14.7 %all-to-all-done = bf16[16,8,32,128]{3,2,1,0:T(8,128)(2,1)S(1)} async-done(((bf16[16,8,32,128]{3,2,1,0:T(8,128)(2,1)}), bf16[16,8,32,128]{3,2,1,0:T(8,128)(2,1)S(1)}, u32[]{:S(2)}, u32[]{:S(2)}) %all-to-all-start) | async-done | bytes 1048608 | tf_op jit(solution)/shard_map/all_to_all | solution.py:210
  34.7 0.1 slice_select_fusion
  34.8 1.9 %collective-permute-start = (bf16[2048,128]{1,0:T(8,128)(2,1)S(1)}, bf16[2048,128]{1,0:T(8,128)(2,1)S(1)}, u32[]{:S(2)}, u32[]{:S(2)}) collective-permute-start(bf16[2048,128]{1,0:T(8,128)(2,1)S(1)} %bitcast.17), channel_id=1, source_target_pairs={{0,8},{8,0},{16,24},{24,16},{32,40},{40,32},{48,56},{56,48},{64,72... | collective-permute-start | bytes 1572872 | tf_op jit(solution)/shard_map/ppermute | solution.py:214
  36.7 1.9 %collective-permute-done.swap_ref = bf16[2048,128]{1,0:T(8,128)(2,1)S(1)} collective-permute-done((bf16[2048,128]{1,0:T(8,128)(2,1)S(1)}, bf16[2048,128]{1,0:T(8,128)(2,1)S(1)}, u32[]{:S(2)}, u32[]{:S(2)}) %collective-permute-start) | collective-permute-done | bytes 524320 | tf_op jit(solution)/shard_map/ppermute | solution.py:214
  38.6 2.8 %shard_map.58 = bf16[8,256,128]{2,1,0:T(8,128)(2,1)} custom-call(s32[1]{0:T(128)} %bitcast.odd_ref, bf16[2,2048,128]{2,1,0:T(8,128)(2,1)S(1)} %bitcast.11, bf16[2048,128]{1,0:T(8,128)(2,1)S(1)} %collective-permute-done.swap_ref), custom_call_target="tpu_custom_call" | custom-call | flops 134217728 | bytes 2097152 | tf_op jit(solution)/shard_map/pallas_call | solution.py:168
  41.4 4.9 %all-to-all-start.2 = ((bf16[8,256,128]{2,1,0:T(8,128)(2,1)}), bf16[8,256,128]{2,1,0:T(8,128)(2,1)S(1)}, u32[]{:S(2)}, u32[]{:S(2)}) async-start(bf16[8,256,128]{2,1,0:T(8,128)(2,1)} %shard_map.58), calls=%async_computation.2 | async-start | bytes 1048576 | tf_op jit(solution)/shard_map/all_to_all | solution.py:195
  46.3 2.8 %shard_map.56 = bf16[8,256,128]{2,1,0:T(8,128)(2,1)} custom-call(s32[1]{0:T(128)} %bitcast.odd_ref, bf16[2,2048,128]{2,1,0:T(8,128)(2,1)S(1)} %bitcast.12, bf16[2048,128]{1,0:T(8,128)(2,1)S(1)} %collective-permute-done.swap_ref), custom_call_target="tpu_custom_call" | custom-call | flops 134217728 | bytes 2097152 | tf_op jit(solution)/shard_map/pallas_call | solution.py:168
  49.1 0.0 copy-start
  49.1 5.8 %all-to-all-done.2 = bf16[8,256,128]{2,1,0:T(8,128)(2,1)S(1)} async-done(((bf16[8,256,128]{2,1,0:T(8,128)(2,1)}), bf16[8,256,128]{2,1,0:T(8,128)(2,1)S(1)}, u32[]{:S(2)}, u32[]{:S(2)}) %all-to-all-start.2) | async-done | bytes 524320 | tf_op jit(solution)/shard_map/all_to_all | solution.py:195
  54.9 5.4 %all-to-all-start.1 = ((bf16[8,256,128]{2,1,0:T(8,128)(2,1)}), bf16[8,256,128]{2,1,0:T(8,128)(2,1)S(1)}, u32[]{:S(2)}, u32[]{:S(2)}) async-start(bf16[8,256,128]{2,1,0:T(8,128)(2,1)} %shard_map.56), calls=%async_computation.1 | async-start | bytes 1048576 | tf_op jit(solution)/shard_map/all_to_all | solution.py:195
  60.3 0.0 copy-done
  60.3 0.7 shard_map.59
  61.0 8.3 %collective-permute-start.1 = (bf16[8,64,128]{2,1,0:T(8,128)(2,1)S(1)}, bf16[8,64,128]{2,1,0:T(8,128)(2,1)S(1)}, u32[]{:S(2)}, u32[]{:S(2)}) collective-permute-start(bf16[8,64,128]{2,1,0:T(8,128)(2,1)S(1)} %shard_map.59), channel_id=1, source_target_pairs={{0,504},{8,0},{16,8},{24,16},{32,24},{40,32},{48,40},{56,48},{64,5... | collective-permute-start | bytes 393224 | tf_op jit(solution)/shard_map/ppermute | solution.py:229
  69.3 0.0 all-to-all-done.1
  69.3 0.7 shard_map.57.first_ref
  70.1 1.8 %collective-permute-done.1.second_ref = bf16[8,64,128]{2,1,0:T(8,128)(2,1)S(1)} collective-permute-done((bf16[8,64,128]{2,1,0:T(8,128)(2,1)S(1)}, bf16[8,64,128]{2,1,0:T(8,128)(2,1)S(1)}, u32[]{:S(2)}, u32[]{:S(2)}) %collective-permute-start.1) | collective-permute-done | bytes 131104 | tf_op jit(solution)/shard_map/ppermute | solution.py:229
  71.8 0.8 %shard_map.60 = f32[8,2,64,128]{3,2,1,0:T(8,128)} custom-call(f32[8,64,128]{2,1,0:T(8,128)S(1)} %shard_map.57.first_ref, bf16[8,64,128]{2,1,0:T(8,128)(2,1)S(1)} %collective-permute-done.1.second_ref), custom_call_target="tpu_custom_call" | custom-call | flops 131072 | bytes 2097152 | tf_op jit(solution)/shard_map/pallas_call | solution.py:168
Async XLA Ops:
  3.7 31.0 %all-to-all-start = ((bf16[16,8,32,128]{3,2,1,0:T(8,128)(2,1)}), bf16[16,8,32,128]{3,2,1,0:T(8,128)(2,1)S(1)}, u32[]{:S(2)}, u32[]{:S(2)}) async-start(bf16[16,8,32,128]{3,2,1,0:T(8,128)(2,1)} %bitcast.15), calls=%async_computation | async-start | bytes 2097152 | tf_op jit(solution)/shard_map/all_to_all | solution.py:210
  34.8 3.8 %collective-permute-start = (bf16[2048,128]{1,0:T(8,128)(2,1)S(1)}, bf16[2048,128]{1,0:T(8,128)(2,1)S(1)}, u32[]{:S(2)}, u32[]{:S(2)}) collective-permute-start(bf16[2048,128]{1,0:T(8,128)(2,1)S(1)} %bitcast.17), channel_id=1, source_target_pairs={{0,8},{8,0},{16,24},{24,16},{32,40},{40,32},{48,56},{56,48},{64,72... | collective-permute-start | bytes 1572872 | tf_op jit(solution)/shard_map/ppermute | solution.py:214
  41.4 13.5 %all-to-all-start.2 = ((bf16[8,256,128]{2,1,0:T(8,128)(2,1)}), bf16[8,256,128]{2,1,0:T(8,128)(2,1)S(1)}, u32[]{:S(2)}, u32[]{:S(2)}) async-start(bf16[8,256,128]{2,1,0:T(8,128)(2,1)} %shard_map.58), calls=%async_computation.2 | async-start | bytes 1048576 | tf_op jit(solution)/shard_map/all_to_all | solution.py:195
  49.1 11.2 %copy-start = (bf16[512,128]{1,0:T(8,128)(2,1)S(1)}, bf16[512,128]{1,0:T(8,128)(2,1)}, u32[]{:S(2)}) copy-start(bf16[512,128]{1,0:T(8,128)(2,1)} %constant.16.clone.table_ref) | copy-start | bytes 393220
  54.9 14.5 %all-to-all-start.1 = ((bf16[8,256,128]{2,1,0:T(8,128)(2,1)}), bf16[8,256,128]{2,1,0:T(8,128)(2,1)S(1)}, u32[]{:S(2)}, u32[]{:S(2)}) async-start(bf16[8,256,128]{2,1,0:T(8,128)(2,1)} %shard_map.56), calls=%async_computation.1 | async-start | bytes 1048576 | tf_op jit(solution)/shard_map/all_to_all | solution.py:195
  61.0 10.8 %collective-permute-start.1 = (bf16[8,64,128]{2,1,0:T(8,128)(2,1)S(1)}, bf16[8,64,128]{2,1,0:T(8,128)(2,1)S(1)}, u32[]{:S(2)}, u32[]{:S(2)}) collective-permute-start(bf16[8,64,128]{2,1,0:T(8,128)(2,1)S(1)} %shard_map.59), channel_id=1, source_target_pairs={{0,504},{8,0},{16,8},{24,16},{32,24},{40,32},{48,40},{56,48},{64,5... | collective-permute-start | bytes 393224 | tf_op jit(solution)/shard_map/ppermute | solution.py:229

commit v4 on v3

--- a/solution.py
+++ b/solution.py
@@ -86,41 +86,62 @@
                 out_ref[to, :, w + 1] = second
 
 
+def left_of(ref, pair):
+    low = low_lanes(DAYS * W)
+    one, other = (ref[pl.ds(2 * pair + f, DAYS * W, stride=FS), :] for f in range(2))
+    both = [jnp.where(low, one, turn(other)), jnp.where(low, turn(one), other)]
+    both = jnp.transpose(jnp.concatenate(both, axis=0)).astype(jnp.bfloat16)
+    return jnp.concatenate([both[:CB], both[CB:]], axis=1)
+
+
+def right_of(ref, pair):
+    low = low_lanes(DAYS * W)
+    parts = []
+    for f in range(2):
+        two = ref[pl.ds(2 * pair + f, DAYS * W, stride=FS), :]
+        parts.append(jnp.concatenate([jnp.where(low, two, -two), turn(two)], axis=0).astype(jnp.bfloat16))
+    return parts
+
+
 def cross_into(out_ref, left, right):
-    low = low_lanes(DAYS * W)
     blank = jnp.zeros((2 * DAYS * W, 2 * CB), jnp.bfloat16)
     for pair in range(FS // 2):
-        rows = [pl.ds(2 * pair + f, DAYS * W, stride=FS) for f in range(2)]
-        one, other = (left[r, :] for r in rows)
-        both = [jnp.where(low, one, turn(other)), jnp.where(low, turn(one), other)]
-        both = jnp.transpose(jnp.concatenate(both, axis=0)).astype(jnp.bfloat16)
-        parts = []
-        for r in rows:
-            two = right[r, :]
-            parts.append(jnp.concatenate([jnp.where(low, two, -two), turn(two)], axis=0).astype(jnp.bfloat16))
-        parts = [jnp.concatenate([parts[0], blank], axis=1), jnp.concatenate([blank, parts[1]], axis=1)]
-        cross = jnp.dot(
-            jnp.concatenate([both[:CB], both[CB:]], axis=1), jnp.concatenate(parts, axis=0),
-            preferred_element_type=jnp.float32,
-        )
+        one, two = right(pair)
+        parts = [jnp.concatenate([one, blank], axis=1), jnp.concatenate([blank, two], axis=1)]
+        cross = jnp.dot(left(pair), jnp.concatenate(parts, axis=0), preferred_element_type=jnp.float32)
         for k in range(DAYS):
             rows = slice(8 * k, 8 * k + 8)
             piece = jnp.concatenate([cross[rows, : 2 * CB], cross[rows, 2 * CB :]], axis=0)
             out_ref[k, pl.ds(16 * pair, 16), :] = piece.astype(jnp.bfloat16)
 
 
-def second_kernel(odd_ref, near_ref, swap_ref, out_ref, left, right):
+def ready_kernel(odd_ref, near_ref, left_ref, right_ref, wide):
     @pl.when(odd_ref[0] == 1)
     def _():
-        left[...] = swap_ref[...].astype(jnp.float32)
-        right[...] = near_ref[1].astype(jnp.float32)
+        wide[...] = near_ref[1].astype(jnp.float32)
+        for pair in range(FS // 2):
+            for f, part in enumerate(right_of(wide, pair)):
+                right_ref[2 * pair + f] = part
 
     @pl.when(odd_ref[0] == 0)
     def _():
-        left[...] = near_ref[0].astype(jnp.float32)
-        right[...] = swap_ref[...].astype(jnp.float32)
-
-    cross_into(out_ref, left, right)
+        wide[...] = near_ref[0].astype(jnp.float32)
+        for pair in range(FS // 2):
+            left_ref[pair] = left_of(wide, pair)
+
+
+def second_kernel(odd_ref, left_ref, right_ref, swap_ref, out_ref, wide):
+    wide[...] = swap_ref[...].astype(jnp.float32)
+
+    @pl.when(odd_ref[0] == 1)
+    def _():
+        cross_into(
+            out_ref, lambda pair: left_of(wide, pair), lambda pair: (right_ref[2 * pair], right_ref[2 * pair + 1])
+        )
+
+    @pl.when(odd_ref[0] == 0)
+    def _():
+        cross_into(out_ref, lambda pair: left_ref[pair], lambda pair: right_of(wide, pair))
 
 
 def first_kernel(odd_ref, near_ref, swap_ref, out_ref, left, right):
@@ -134,7 +155,7 @@
         left[...] = near_ref[1].astype(jnp.float32)
         right[...] = swap_ref[...].astype(jnp.float32)
 
-    cross_into(out_ref, left, right)
+    cross_into(out_ref, lambda pair: left_of(left, pair), lambda pair: right_of(right, pair))
 
 
 def lags_of(wide, table):
@@ -156,20 +177,31 @@
         out_ref[rows] = lags.astype(out_ref.dtype)
 
 
-def join_kernel(first_ref, second_ref, out_ref):
-    out_ref[:, 0] = first_ref[...]
-    out_ref[:, 1] = second_ref[...].astype(jnp.float32)
-
-
-def call(kernel, out_shape, dtype, scratch, flops, *args, scalars=0, space=pltpu.VMEM, limit=VMEM):
+def first_lag_kernel(cross_ref, table_ref, out_hbm, wide, stage, sems):
+    wide[...] = cross_ref[...].astype(jnp.float32)
+    copies = []
+    for at, (rows, lags) in enumerate(lags_of(wide, table_ref[...])):
+        stage[rows] = lags
+        copies.append(pltpu.make_async_copy(stage.at[rows], out_hbm.at[rows, 0], sems.at[at]))
+        copies[-1].start()
+    for copy in copies:
+        copy.wait()
+
+
+def second_into_kernel(second_ref, held_hbm, out_hbm, stage, sem):
+    stage[...] = second_ref[...].astype(jnp.float32)
+    copy = pltpu.make_async_copy(stage, out_hbm.at[:, 1], sem)
+    copy.start()
+    copy.wait()
+
+
+def call(kernel, out_shape, dtype, scratch, flops, *args, scalars=0, space=pltpu.VMEM, out_space=pltpu.VMEM, limit=VMEM):
     smem = [pl.BlockSpec(memory_space=pltpu.SMEM)] * scalars
-    if dtype is not None:
-        out_shape = jax.ShapeDtypeStruct(out_shape, dtype)
     return pl.pallas_call(
         kernel,
-        out_shape=out_shape,
+        out_shape=jax.ShapeDtypeStruct(out_shape, dtype),
         in_specs=smem + [pl.BlockSpec(memory_space=space)] * (len(args) - scalars),
-        out_specs=jax.tree.map(lambda _: pl.BlockSpec(memory_space=pltpu.VMEM), out_shape),
+        out_specs=pl.BlockSpec(memory_space=out_space),
         scratch_shapes=scratch,
         compiler_params=pltpu.CompilerParams(vmem_limit_bytes=limit),
         cost_estimate=pl.CostEstimate(flops=flops, bytes_accessed=2 << 20, transcendentals=0),
@@ -213,22 +245,47 @@
     mine = jnp.where(odd == 1, near[0], near[1])
     swap = lax.ppermute(mine, "chan", [(b, b ^ 1) for b in range(blocks)])
 
-    def cross(kernel):
-        return call(
-            kernel, (DAYS, FS * 8, 2 * CB), jnp.bfloat16, [WHOLE] * 2, FS * UNIT_FLOPS, flag, near, swap, scalars=1
+    shape = (DAYS, FS * 8, 2 * CB)
+    left, right = pl.pallas_call(
+        ready_kernel,
+        out_shape=[
+            jax.ShapeDtypeStruct((FS // 2, CB, 4 * CB), jnp.bfloat16),
+            jax.ShapeDtypeStruct((FS, 2 * CB, 2 * CB), jnp.bfloat16),
+        ],
+        in_specs=[pl.BlockSpec(memory_space=pltpu.SMEM), pl.BlockSpec(memory_space=pltpu.VMEM)],
+        out_specs=[pl.BlockSpec(memory_space=pltpu.VMEM)] * 2,
+        scratch_shapes=[WHOLE],
+        compiler_params=pltpu.CompilerParams(vmem_limit_bytes=VMEM),
+        cost_estimate=pl.CostEstimate(flops=1 << 20, bytes_accessed=2 << 20, transcendentals=0),
+    )(flag, near)
+    second = exchange(
+        call(
+            second_kernel, shape, jnp.bfloat16, [WHOLE], FS * UNIT_FLOPS, flag, left, right, swap, scalars=1
         )
-
-    def lags(pairs, dtype):
-        return call(
-            lag_kernel, (8, CB, L), dtype, [WHOLE], LAG_FLOPS, pairs.reshape(F * 8, 2 * CB), table
-        )
-
-    second = exchange(cross(second_kernel))
-    first = exchange(cross(first_kernel))
-    second = lags(second, jnp.bfloat16)
+    )
+    first = exchange(
+        call(first_kernel, shape, jnp.bfloat16, [WHOLE] * 2, FS * UNIT_FLOPS, flag, near, swap, scalars=1)
+    )
+
+    second = call(
+        lag_kernel, (8, CB, L), jnp.bfloat16, [WHOLE], LAG_FLOPS, second.reshape(F * 8, 2 * CB), table
+    )
     second = lax.ppermute(second, "chan", [(b, (b - 1) % blocks) for b in range(blocks)])
-    first = lags(first, jnp.float32)
-    return call(join_kernel, (8, 2, CB, L), jnp.float32, [], 1 << 17, first, second)
+    stage = pltpu.VMEM((8, CB, L), jnp.float32)
+    first = call(
+        first_lag_kernel, (8, 2, CB, L), jnp.float32, [WHOLE, stage, pltpu.SemaphoreType.DMA((4,))], LAG_FLOPS,
+        first.reshape(F * 8, 2 * CB), table, out_space=pltpu.HBM,
+    )
+    return pl.pallas_call(
+        second_into_kernel,
+        out_shape=jax.ShapeDtypeStruct((8, 2, CB, L), jnp.float32),
+        in_specs=[pl.BlockSpec(memory_space=pltpu.VMEM), pl.BlockSpec(memory_space=pltpu.HBM)],
+        out_specs=pl.BlockSpec(memory_space=pltpu.HBM),
+        scratch_shapes=[stage, pltpu.SemaphoreType.DMA],
+        input_output_aliases={1: 0},
+        compiler_params=pltpu.CompilerParams(vmem_limit_bytes=VMEM),
+        cost_estimate=pl.CostEstimate(flops=1 << 17, bytes_accessed=1 << 18, transcendentals=0),
+    )(second, first)
 
 
 def solution(mesh):

time: 73.1 us -> 72.9 us (level)
  waiting for transfers between devices: 24.1 us -> 22.8 us
    ppermute x1, waiting for transfers between devices: 1.88 us -> 0.79 us  [shards(): swap = lax.ppermute(mine, 'chan', [(b, b ^ 1) for b in range(blocks)])]
    pallas_call x6 -> x7, Pallas kernels: 11.5 us -> 12.1 us  [the longest x5 10.3 us: call(): pl.pallas_call(kernel, out_shape=jax.ShapeDtypeStruct(out_shape, dtype),...]
  transfers between devices with their start and end apart: 5 -> 5, of which waited for: 4 -> 4; matrix products, arithmetic and copies ran while one was open for 0% -> 0% of each run, Pallas kernels for 6% -> 8%
where the time goes in v4:
time: 72.9 us; the launch traced here: 72.5 us
  starting transfers between devices  37.4 us (51%)
  waiting for transfers between devices  22.8 us (31%)
  Pallas kernels  12.1 us (17%)
    all_to_all x1, starting transfers between devices, shards(): lax.all_to_all(spectra.reshape(2 * DAYS, W, FS, 2 * CB), ('chan', 'day'),...  16.3 us
    all_to_all x1, waiting for transfers between devices, shards(): lax.all_to_all(spectra.reshape(2 * DAYS, W, FS, 2 * CB), ('chan', 'day'),...  14.7 us
    pallas_call x5, Pallas kernels, call(): pl.pallas_call(kernel, out_shape=jax.ShapeDtypeStruct(out_shape, dtype),...  10.3 us
    all_to_all x2, starting transfers between devices, exchange(): return lax.all_to_all(v, 'day', 0, 0, tiled=True)  10.2 us
    ppermute x1, starting transfers between devices, shards(): lax.ppermute(second, 'chan', [(b, (b - 1) % blocks) for b in range(blocks)])  8.98 us
    all_to_all x2, waiting for transfers between devices, exchange(): return lax.all_to_all(v, 'day', 0, 0, tiled=True)  6.27 us
    ppermute x1, starting transfers between devices, shards(): swap = lax.ppermute(mine, 'chan', [(b, b ^ 1) for b in range(blocks)])  1.92 us
  transfers between devices with their start and end apart: 5, of which 4 were waited for; matrix products, arithmetic and copies ran while one was open for 0% of the time, Pallas kernels for 8%

profile of v4, /device:TPU:2, one launch (start us, length us, event | category | flops | bytes accessed | tf_op | source)
XLA Modules:
  0.0 72.5 jit_solution(8723592626341833853)
XLA Ops:
  0.0 3.7 %shard_map.55 = bf16[2,8,8,32,128]{4,3,2,1,0:T(8,128)(2,1)} custom-call(bf16[512,1024]{1,0:T(8,128)(2,1)} %bitcast.16, s32[8,64]{1,0:T(8,128)} %bitcast.18, f32[1,256]{1,0:T(1,128)} %bitcast.19, bf16[512,1024]{1,0:T(8,128)(2,1)} %constant.17.clone.table_hbm), custom_call_target="tpu_custom_call" | custom-call | flops 536870912 | bytes 2097152 | tf_op jit(solution)/shard_map/pallas_call | solution.py:200
  3.7 16.3 %all-to-all-start = ((bf16[16,8,32,128]{3,2,1,0:T(8,128)(2,1)}), bf16[16,8,32,128]{3,2,1,0:T(8,128)(2,1)S(1)}, u32[]{:S(2)}, u32[]{:S(2)}) async-start(bf16[16,8,32,128]{3,2,1,0:T(8,128)(2,1)} %bitcast.15), calls=%async_computation | async-start | bytes 2097152 | tf_op jit(solution)/shard_map/all_to_all | solution.py:242
  20.0 14.7 %all-to-all-done = bf16[16,8,32,128]{3,2,1,0:T(8,128)(2,1)S(1)} async-done(((bf16[16,8,32,128]{3,2,1,0:T(8,128)(2,1)}), bf16[16,8,32,128]{3,2,1,0:T(8,128)(2,1)S(1)}, u32[]{:S(2)}, u32[]{:S(2)}) %all-to-all-start) | async-done | bytes 1048608 | tf_op jit(solution)/shard_map/all_to_all | solution.py:242
  34.7 0.1 slice_select_fusion
  34.7 1.9 %collective-permute-start = (bf16[2048,128]{1,0:T(8,128)(2,1)S(1)}, bf16[2048,128]{1,0:T(8,128)(2,1)S(1)}, u32[]{:S(2)}, u32[]{:S(2)}) collective-permute-start(bf16[2048,128]{1,0:T(8,128)(2,1)S(1)} %bitcast.17), channel_id=1, source_target_pairs={{0,8},{8,0},{16,24},{24,16},{32,40},{40,32},{48,56},{56,48},{64,72... | collective-permute-start | bytes 1572872 | tf_op jit(solution)/shard_map/ppermute | solution.py:246
  36.7 1.1 %shard_map.56 = (bf16[16,64,256]{2,1,0:T(8,128)(2,1)S(1)}, bf16[32,128,128]{2,1,0:T(8,128)(2,1)S(1)}) custom-call(s32[1]{0:T(128)} %bitcast.odd_ref, bf16[2,2048,128]{2,1,0:T(8,128)(2,1)S(1)} %bitcast.11), custom_call_target="tpu_custom_call" | custom-call | flops 1048576 | bytes 2097152 | tf_op jit(solution)/shard_map/pallas_call | solution.py:249
  37.8 0.8 %collective-permute-done.swap_ref = bf16[2048,128]{1,0:T(8,128)(2,1)S(1)} collective-permute-done((bf16[2048,128]{1,0:T(8,128)(2,1)S(1)}, bf16[2048,128]{1,0:T(8,128)(2,1)S(1)}, u32[]{:S(2)}, u32[]{:S(2)}) %collective-permute-start) | collective-permute-done | bytes 524320 | tf_op jit(solution)/shard_map/ppermute | solution.py:246
  38.6 1.8 %shard_map.57 = bf16[8,256,128]{2,1,0:T(8,128)(2,1)} custom-call(s32[1]{0:T(128)} %bitcast.odd_ref, bf16[16,64,256]{2,1,0:T(8,128)(2,1)S(1)} %get-tuple-element.7.left_ref, bf16[32,128,128]{2,1,0:T(8,128)(2,1)S(1)} %get-tuple-element.8.right_ref, bf16[2048,128]{1,0:T(8,128)(2,1)S(1)} %collective-permute-done.swap_ref), custom_call_target="tpu_custom_call" | custom-call | flops 134217728 | bytes 2097152 | tf_op jit(solution)/shard_map/pallas_call | solution.py:200
  40.3 4.9 %all-to-all-start.1 = ((bf16[8,256,128]{2,1,0:T(8,128)(2,1)}), bf16[8,256,128]{2,1,0:T(8,128)(2,1)S(1)}, u32[]{:S(2)}, u32[]{:S(2)}) async-start(bf16[8,256,128]{2,1,0:T(8,128)(2,1)} %shard_map.57), calls=%async_computation.1 | async-start | bytes 1048576 | tf_op jit(solution)/shard_map/all_to_all | solution.py:227
  45.2 2.8 %shard_map.59 = bf16[8,256,128]{2,1,0:T(8,128)(2,1)} custom-call(s32[1]{0:T(128)} %bitcast.odd_ref, bf16[2,2048,128]{2,1,0:T(8,128)(2,1)S(1)} %bitcast.12, bf16[2048,128]{1,0:T(8,128)(2,1)S(1)} %collective-permute-done.swap_ref), custom_call_target="tpu_custom_call" | custom-call | flops 134217728 | bytes 2097152 | tf_op jit(solution)/shard_map/pallas_call | solution.py:200
  48.0 0.0 copy-start
  48.0 6.3 %all-to-all-done.1 = bf16[8,256,128]{2,1,0:T(8,128)(2,1)S(1)} async-done(((bf16[8,256,128]{2,1,0:T(8,128)(2,1)}), bf16[8,256,128]{2,1,0:T(8,128)(2,1)S(1)}, u32[]{:S(2)}, u32[]{:S(2)}) %all-to-all-start.1) | async-done | bytes 524320 | tf_op jit(solution)/shard_map/all_to_all | solution.py:227
  54.2 5.3 %all-to-all-start.2 = ((bf16[8,256,128]{2,1,0:T(8,128)(2,1)}), bf16[8,256,128]{2,1,0:T(8,128)(2,1)S(1)}, u32[]{:S(2)}, u32[]{:S(2)}) async-start(bf16[8,256,128]{2,1,0:T(8,128)(2,1)} %shard_map.59), calls=%async_computation.2 | async-start | bytes 1048576 | tf_op jit(solution)/shard_map/all_to_all | solution.py:227
  59.6 0.0 copy-done
  59.6 0.7 shard_map.58
  60.3 9.0 %collective-permute-start.1 = (bf16[8,64,128]{2,1,0:T(8,128)(2,1)S(1)}, bf16[8,64,128]{2,1,0:T(8,128)(2,1)S(1)}, u32[]{:S(2)}, u32[]{:S(2)}) collective-permute-start(bf16[8,64,128]{2,1,0:T(8,128)(2,1)S(1)} %shard_map.58), channel_id=1, source_target_pairs={{0,504},{8,0},{16,8},{24,16},{32,24},{40,32},{48,40},{56,48},{64,5... | collective-permute-start | bytes 393224 | tf_op jit(solution)/shard_map/ppermute | solution.py:273
  69.3 0.0 all-to-all-done.2
  69.3 1.4 %shard_map.60.held_hbm = f32[8,2,64,128]{3,2,1,0:T(8,128)} custom-call(bf16[2048,128]{1,0:T(8,128)(2,1)S(1)} %bitcast.14, bf16[512,128]{1,0:T(8,128)(2,1)S(1)} %copy-done), custom_call_target="tpu_custom_call" | custom-call | flops 67108864 | bytes 2097152 | tf_op jit(solution)/shard_map/pallas_call | solution.py:200
  70.6 1.1 %collective-permute-done.1.second_ref = bf16[8,64,128]{2,1,0:T(8,128)(2,1)S(1)} collective-permute-done((bf16[8,64,128]{2,1,0:T(8,128)(2,1)S(1)}, bf16[8,64,128]{2,1,0:T(8,128)(2,1)S(1)}, u32[]{:S(2)}, u32[]{:S(2)}) %collective-permute-start.1) | collective-permute-done | bytes 131104 | tf_op jit(solution)/shard_map/ppermute | solution.py:273
  71.8 0.7 %shard_map.61 = f32[8,2,64,128]{3,2,1,0:T(8,128)} custom-call(bf16[8,64,128]{2,1,0:T(8,128)(2,1)S(1)} %collective-permute-done.1.second_ref, f32[8,2,64,128]{3,2,1,0:T(8,128)} %shard_map.60.held_hbm), custom_call_target="tpu_custom_call", output_to_operand_aliasing={{}: (1, {})} | custom-call | flops 131072 | bytes 262144 | tf_op jit(solution)/shard_map/pallas_call | solution.py:279
Async XLA Ops:
  3.7 31.0 %all-to-all-start = ((bf16[16,8,32,128]{3,2,1,0:T(8,128)(2,1)}), bf16[16,8,32,128]{3,2,1,0:T(8,128)(2,1)S(1)}, u32[]{:S(2)}, u32[]{:S(2)}) async-start(bf16[16,8,32,128]{3,2,1,0:T(8,128)(2,1)} %bitcast.15), calls=%async_computation | async-start | bytes 2097152 | tf_op jit(solution)/shard_map/all_to_all | solution.py:242
  34.7 3.8 %collective-permute-start = (bf16[2048,128]{1,0:T(8,128)(2,1)S(1)}, bf16[2048,128]{1,0:T(8,128)(2,1)S(1)}, u32[]{:S(2)}, u32[]{:S(2)}) collective-permute-start(bf16[2048,128]{1,0:T(8,128)(2,1)S(1)} %bitcast.17), channel_id=1, source_target_pairs={{0,8},{8,0},{16,24},{24,16},{32,40},{40,32},{48,56},{56,48},{64,72... | collective-permute-start | bytes 1572872 | tf_op jit(solution)/shard_map/ppermute | solution.py:246
  40.3 13.9 %all-to-all-start.1 = ((bf16[8,256,128]{2,1,0:T(8,128)(2,1)}), bf16[8,256,128]{2,1,0:T(8,128)(2,1)S(1)}, u32[]{:S(2)}, u32[]{:S(2)}) async-start(bf16[8,256,128]{2,1,0:T(8,128)(2,1)} %shard_map.57), calls=%async_computation.1 | async-start | bytes 1048576 | tf_op jit(solution)/shard_map/all_to_all | solution.py:227
  48.0 11.6 %copy-start = (bf16[512,128]{1,0:T(8,128)(2,1)S(1)}, bf16[512,128]{1,0:T(8,128)(2,1)}, u32[]{:S(2)}) copy-start(bf16[512,128]{1,0:T(8,128)(2,1)} %constant.16.clone.table_ref) | copy-start | bytes 393220
  54.2 15.0 %all-to-all-start.2 = ((bf16[8,256,128]{2,1,0:T(8,128)(2,1)}), bf16[8,256,128]{2,1,0:T(8,128)(2,1)S(1)}, u32[]{:S(2)}, u32[]{:S(2)}) async-start(bf16[8,256,128]{2,1,0:T(8,128)(2,1)} %shard_map.59), calls=%async_computation.2 | async-start | bytes 1048576 | tf_op jit(solution)/shard_map/all_to_all | solution.py:227
  60.3 11.5 %collective-permute-start.1 = (bf16[8,64,128]{2,1,0:T(8,128)(2,1)S(1)}, bf16[8,64,128]{2,1,0:T(8,128)(2,1)S(1)}, u32[]{:S(2)}, u32[]{:S(2)}) collective-permute-start(bf16[8,64,128]{2,1,0:T(8,128)(2,1)S(1)} %shard_map.58), channel_id=1, source_target_pairs={{0,504},{8,0},{16,8},{24,16},{32,24},{40,32},{48,40},{56,48},{64,5... | collective-permute-start | bytes 393224 | tf_op jit(solution)/shard_map/ppermute | solution.py:273

commit v5 on v4

--- a/solution.py
+++ b/solution.py
@@ -46,7 +46,7 @@
 def spectra_kernel(x_hbm, good_hbm, resp_hbm, table_hbm, out_ref, x_ref, good_ref, resp_ref, table_ref, xs, normed, sems):
     part = CB // PARTS
     pairs = [(x_hbm.at[pl.ds(p * part * W, part * W)], x_ref.at[pl.ds(p * part * W, part * W)]) for p in range(PARTS)]
-    pairs += [(good_hbm, good_ref), (resp_hbm, resp_ref), (table_hbm, table_ref)]
+    pairs += [(good_hbm, good_ref), (resp_hbm, resp_ref), (table_hbm, table_ref.at[:, pl.ds(0, S // 2)])]
     copies = [pltpu.make_async_copy(source, target, sems.at[at]) for at, (source, target) in enumerate(pairs)]
     for copy in copies:
         copy.start()
@@ -64,6 +64,9 @@
             normed[pl.ds(w * CB + p * part, part), :] = scaled
     for copy in copies[PARTS:]:
         copy.wait()
+    half = table_ref[:, : S // 2]
+    flip = lax.broadcasted_iota(jnp.int32, half.shape, 0) % 2 == 1
+    table_ref[:, S // 2 :] = jnp.where(flip, -half.astype(jnp.float32), half.astype(jnp.float32)).astype(jnp.bfloat16)
     gain = jnp.transpose(jnp.broadcast_to(resp_ref[...], (2 * CB, F)))
     low = low_lanes(F)
     good = good_ref[...].astype(jnp.float32)
@@ -214,8 +217,8 @@
 
 
 def spectra_call(x, good, response):
-    operands = (x, good, response, jnp.asarray(dft_table()))
-    scratch = [pltpu.VMEM(v.shape, v.dtype) for v in operands]
+    operands = (x, good, response, jnp.asarray(dft_table()[:, : S // 2]))
+    scratch = [pltpu.VMEM(v.shape, v.dtype) for v in operands[:3]] + [pltpu.VMEM((2 * F, S), jnp.bfloat16)]
     scratch += [pltpu.VMEM((S // 128, CB * W, 128), jnp.float32), pltpu.VMEM((CB * W, S), jnp.bfloat16)]
     return call(
         spectra_kernel, (2, DAYS, W, FS, 2 * CB), jnp.bfloat16, scratch + [pltpu.SemaphoreType.DMA((PARTS + 3,))],

time: 72.9 us -> 72.9 us (level)
  no operation moved by 1% of the time
where the time goes in v5:
time: 72.9 us; the launch traced here: 72.5 us
  starting transfers between devices  37.4 us (51%)
  waiting for transfers between devices  22.8 us (31%)
  Pallas kernels  12.1 us (17%)
    all_to_all x1, starting transfers between devices, shards(): lax.all_to_all(spectra.reshape(2 * DAYS, W, FS, 2 * CB), ('chan', 'day'),...  16.3 us
    all_to_all x1, waiting for transfers between devices, shards(): lax.all_to_all(spectra.reshape(2 * DAYS, W, FS, 2 * CB), ('chan', 'day'),...  14.7 us
    pallas_call x5, Pallas kernels, call(): pl.pallas_call(kernel, out_shape=jax.ShapeDtypeStruct(out_shape, dtype),...  10.3 us
    all_to_all x2, starting transfers between devices, exchange(): return lax.all_to_all(v, 'day', 0, 0, tiled=True)  10.2 us
    ppermute x1, starting transfers between devices, shards(): lax.ppermute(second, 'chan', [(b, (b - 1) % blocks) for b in range(blocks)])  8.98 us
    all_to_all x2, waiting for transfers between devices, exchange(): return lax.all_to_all(v, 'day', 0, 0, tiled=True)  6.27 us
    ppermute x1, starting transfers between devices, shards(): swap = lax.ppermute(mine, 'chan', [(b, b ^ 1) for b in range(blocks)])  1.92 us
  transfers between devices with their start and end apart: 5, of which 4 were waited for; matrix products, arithmetic and copies ran while one was open for 0% of the time, Pallas kernels for 8%

profile of v5, /device:TPU:2, one launch (start us, length us, event | category | flops | bytes accessed | tf_op | source)
XLA Modules:
  0.0 72.5 jit_solution(16438135416364047769)
XLA Ops:
  0.0 3.7 %shard_map.55 = bf16[2,8,8,32,128]{4,3,2,1,0:T(8,128)(2,1)} custom-call(bf16[512,1024]{1,0:T(8,128)(2,1)} %bitcast.16, s32[8,64]{1,0:T(8,128)} %bitcast.18, f32[1,256]{1,0:T(1,128)} %bitcast.19, bf16[512,512]{1,0:T(8,128)(2,1)} %constant.17.clone.table_hbm), custom_call_target="tpu_custom_call" | custom-call | flops 536870912 | bytes 2097152 | tf_op jit(solution)/shard_map/pallas_call | solution.py:203
  3.7 16.3 %all-to-all-start = ((bf16[16,8,32,128]{3,2,1,0:T(8,128)(2,1)}), bf16[16,8,32,128]{3,2,1,0:T(8,128)(2,1)S(1)}, u32[]{:S(2)}, u32[]{:S(2)}) async-start(bf16[16,8,32,128]{3,2,1,0:T(8,128)(2,1)} %bitcast.15), calls=%async_computation | async-start | bytes 2097152 | tf_op jit(solution)/shard_map/all_to_all | solution.py:245
  20.0 14.7 %all-to-all-done = bf16[16,8,32,128]{3,2,1,0:T(8,128)(2,1)S(1)} async-done(((bf16[16,8,32,128]{3,2,1,0:T(8,128)(2,1)}), bf16[16,8,32,128]{3,2,1,0:T(8,128)(2,1)S(1)}, u32[]{:S(2)}, u32[]{:S(2)}) %all-to-all-start) | async-done | bytes 1048608 | tf_op jit(solution)/shard_map/all_to_all | solution.py:245
  34.7 0.1 slice_select_fusion
  34.7 1.9 %collective-permute-start = (bf16[2048,128]{1,0:T(8,128)(2,1)S(1)}, bf16[2048,128]{1,0:T(8,128)(2,1)S(1)}, u32[]{:S(2)}, u32[]{:S(2)}) collective-permute-start(bf16[2048,128]{1,0:T(8,128)(2,1)S(1)} %bitcast.17), channel_id=1, source_target_pairs={{0,8},{8,0},{16,24},{24,16},{32,40},{40,32},{48,56},{56,48},{64,72... | collective-permute-start | bytes 1572872 | tf_op jit(solution)/shard_map/ppermute | solution.py:249
  36.7 1.1 %shard_map.56 = (bf16[16,64,256]{2,1,0:T(8,128)(2,1)S(1)}, bf16[32,128,128]{2,1,0:T(8,128)(2,1)S(1)}) custom-call(s32[1]{0:T(128)} %bitcast.odd_ref, bf16[2,2048,128]{2,1,0:T(8,128)(2,1)S(1)} %bitcast.11), custom_call_target="tpu_custom_call" | custom-call | flops 1048576 | bytes 2097152 | tf_op jit(solution)/shard_map/pallas_call | solution.py:252
  37.8 0.8 %collective-permute-done.swap_ref = bf16[2048,128]{1,0:T(8,128)(2,1)S(1)} collective-permute-done((bf16[2048,128]{1,0:T(8,128)(2,1)S(1)}, bf16[2048,128]{1,0:T(8,128)(2,1)S(1)}, u32[]{:S(2)}, u32[]{:S(2)}) %collective-permute-start) | collective-permute-done | bytes 524320 | tf_op jit(solution)/shard_map/ppermute | solution.py:249
  38.5 1.8 %shard_map.57 = bf16[8,256,128]{2,1,0:T(8,128)(2,1)} custom-call(s32[1]{0:T(128)} %bitcast.odd_ref, bf16[16,64,256]{2,1,0:T(8,128)(2,1)S(1)} %get-tuple-element.7.left_ref, bf16[32,128,128]{2,1,0:T(8,128)(2,1)S(1)} %get-tuple-element.8.right_ref, bf16[2048,128]{1,0:T(8,128)(2,1)S(1)} %collective-permute-done.swap_ref), custom_call_target="tpu_custom_call" | custom-call | flops 134217728 | bytes 2097152 | tf_op jit(solution)/shard_map/pallas_call | solution.py:203
  40.3 4.9 %all-to-all-start.1 = ((bf16[8,256,128]{2,1,0:T(8,128)(2,1)}), bf16[8,256,128]{2,1,0:T(8,128)(2,1)S(1)}, u32[]{:S(2)}, u32[]{:S(2)}) async-start(bf16[8,256,128]{2,1,0:T(8,128)(2,1)} %shard_map.57), calls=%async_computation.1 | async-start | bytes 1048576 | tf_op jit(solution)/shard_map/all_to_all | solution.py:230
  45.2 2.8 %shard_map.59 = bf16[8,256,128]{2,1,0:T(8,128)(2,1)} custom-call(s32[1]{0:T(128)} %bitcast.odd_ref, bf16[2,2048,128]{2,1,0:T(8,128)(2,1)S(1)} %bitcast.12, bf16[2048,128]{1,0:T(8,128)(2,1)S(1)} %collective-permute-done.swap_ref), custom_call_target="tpu_custom_call" | custom-call | flops 134217728 | bytes 2097152 | tf_op jit(solution)/shard_map/pallas_call | solution.py:203
  48.0 0.0 copy-start
  48.0 6.3 %all-to-all-done.1 = bf16[8,256,128]{2,1,0:T(8,128)(2,1)S(1)} async-done(((bf16[8,256,128]{2,1,0:T(8,128)(2,1)}), bf16[8,256,128]{2,1,0:T(8,128)(2,1)S(1)}, u32[]{:S(2)}, u32[]{:S(2)}) %all-to-all-start.1) | async-done | bytes 524320 | tf_op jit(solution)/shard_map/all_to_all | solution.py:230
  54.2 5.3 %all-to-all-start.2 = ((bf16[8,256,128]{2,1,0:T(8,128)(2,1)}), bf16[8,256,128]{2,1,0:T(8,128)(2,1)S(1)}, u32[]{:S(2)}, u32[]{:S(2)}) async-start(bf16[8,256,128]{2,1,0:T(8,128)(2,1)} %shard_map.59), calls=%async_computation.2 | async-start | bytes 1048576 | tf_op jit(solution)/shard_map/all_to_all | solution.py:230
  59.5 0.0 copy-done
  59.6 0.7 shard_map.58
  60.3 9.0 %collective-permute-start.1 = (bf16[8,64,128]{2,1,0:T(8,128)(2,1)S(1)}, bf16[8,64,128]{2,1,0:T(8,128)(2,1)S(1)}, u32[]{:S(2)}, u32[]{:S(2)}) collective-permute-start(bf16[8,64,128]{2,1,0:T(8,128)(2,1)S(1)} %shard_map.58), channel_id=1, source_target_pairs={{0,504},{8,0},{16,8},{24,16},{32,24},{40,32},{48,40},{56,48},{64,5... | collective-permute-start | bytes 393224 | tf_op jit(solution)/shard_map/ppermute | solution.py:276
  69.2 0.0 all-to-all-done.2
  69.3 1.4 %shard_map.60.held_hbm = f32[8,2,64,128]{3,2,1,0:T(8,128)} custom-call(bf16[2048,128]{1,0:T(8,128)(2,1)S(1)} %bitcast.14, bf16[512,128]{1,0:T(8,128)(2,1)S(1)} %copy-done), custom_call_target="tpu_custom_call" | custom-call | flops 67108864 | bytes 2097152 | tf_op jit(solution)/shard_map/pallas_call | solution.py:203
  70.6 1.1 %collective-permute-done.1.second_ref = bf16[8,64,128]{2,1,0:T(8,128)(2,1)S(1)} collective-permute-done((bf16[8,64,128]{2,1,0:T(8,128)(2,1)S(1)}, bf16[8,64,128]{2,1,0:T(8,128)(2,1)S(1)}, u32[]{:S(2)}, u32[]{:S(2)}) %collective-permute-start.1) | collective-permute-done | bytes 131104 | tf_op jit(solution)/shard_map/ppermute | solution.py:276
  71.7 0.7 %shard_map.61 = f32[8,2,64,128]{3,2,1,0:T(8,128)} custom-call(bf16[8,64,128]{2,1,0:T(8,128)(2,1)S(1)} %collective-permute-done.1.second_ref, f32[8,2,64,128]{3,2,1,0:T(8,128)} %shard_map.60.held_hbm), custom_call_target="tpu_custom_call", output_to_operand_aliasing={{}: (1, {})} | custom-call | flops 131072 | bytes 262144 | tf_op jit(solution)/shard_map/pallas_call | solution.py:282
Async XLA Ops:
  3.7 31.0 %all-to-all-start = ((bf16[16,8,32,128]{3,2,1,0:T(8,128)(2,1)}), bf16[16,8,32,128]{3,2,1,0:T(8,128)(2,1)S(1)}, u32[]{:S(2)}, u32[]{:S(2)}) async-start(bf16[16,8,32,128]{3,2,1,0:T(8,128)(2,1)} %bitcast.15), calls=%async_computation | async-start | bytes 2097152 | tf_op jit(solution)/shard_map/all_to_all | solution.py:245
  34.7 3.8 %collective-permute-start = (bf16[2048,128]{1,0:T(8,128)(2,1)S(1)}, bf16[2048,128]{1,0:T(8,128)(2,1)S(1)}, u32[]{:S(2)}, u32[]{:S(2)}) collective-permute-start(bf16[2048,128]{1,0:T(8,128)(2,1)S(1)} %bitcast.17), channel_id=1, source_target_pairs={{0,8},{8,0},{16,24},{24,16},{32,40},{40,32},{48,56},{56,48},{64,72... | collective-permute-start | bytes 1572872 | tf_op jit(solution)/shard_map/ppermute | solution.py:249
  40.3 13.9 %all-to-all-start.1 = ((bf16[8,256,128]{2,1,0:T(8,128)(2,1)}), bf16[8,256,128]{2,1,0:T(8,128)(2,1)S(1)}, u32[]{:S(2)}, u32[]{:S(2)}) async-start(bf16[8,256,128]{2,1,0:T(8,128)(2,1)} %shard_map.57), calls=%async_computation.1 | async-start | bytes 1048576 | tf_op jit(solution)/shard_map/all_to_all | solution.py:230
  48.0 11.6 %copy-start = (bf16[512,128]{1,0:T(8,128)(2,1)S(1)}, bf16[512,128]{1,0:T(8,128)(2,1)}, u32[]{:S(2)}) copy-start(bf16[512,128]{1,0:T(8,128)(2,1)} %constant.16.clone.table_ref) | copy-start | bytes 393220
  54.2 15.0 %all-to-all-start.2 = ((bf16[8,256,128]{2,1,0:T(8,128)(2,1)}), bf16[8,256,128]{2,1,0:T(8,128)(2,1)S(1)}, u32[]{:S(2)}, u32[]{:S(2)}) async-start(bf16[8,256,128]{2,1,0:T(8,128)(2,1)} %shard_map.59), calls=%async_computation.2 | async-start | bytes 1048576 | tf_op jit(solution)/shard_map/all_to_all | solution.py:230
  60.3 11.5 %collective-permute-start.1 = (bf16[8,64,128]{2,1,0:T(8,128)(2,1)S(1)}, bf16[8,64,128]{2,1,0:T(8,128)(2,1)S(1)}, u32[]{:S(2)}, u32[]{:S(2)}) collective-permute-start(bf16[8,64,128]{2,1,0:T(8,128)(2,1)S(1)} %shard_map.58), channel_id=1, source_target_pairs={{0,504},{8,0},{16,8},{24,16},{32,24},{40,32},{48,40},{56,48},{64,5... | collective-permute-start | bytes 393224 | tf_op jit(solution)/shard_map/ppermute | solution.py:276
